TPU v7x, 256 devices: a whole 4x4x8 slice. The times are simulated.
256 devices in a mesh: maprow: 16 (over x, y), mapcol: 8 (over z), sect: 2 (over core).
Axes of the slice: x: 4, y: 4, z: 8, core: 2. Of those that a mesh axis runs over, the one named last changes fastest.
Arguments:
- elevation: float32 [4096, 8192], P('maprow', ('mapcol', 'sect')), may hold values from -60 to 60
- layover: int32 [4096, 8192], P('maprow', ('mapcol', 'sect')), may hold values 0 or 1
- footprint_pixel: int32 [4096, 8192], P('maprow', ('mapcol', 'sect')), may hold values from 0 to 127
- footprint_device: int32 [256, 512, 1], P(('maprow', 'mapcol', 'sect')), may hold values from 0 to 127; in each aligned block of 512 rows (0 to 511, 512 to 1023, ..., all dimensions but the last counted through in order) at most 8 rows name the same one
- local_block: int32 [256, 512], P(('maprow', 'mapcol', 'sect')), may hold values from 0 to 127
- backscatter: float32 [32768, 128], P(('maprow', 'mapcol', 'sect')), may hold values from 0.5 to 8
Outputs:
- gamma_radar: float32 [32768, 128], P(('maprow', 'mapcol', 'sect'))
- gamma_map: float32 [4096, 8192], P('maprow', ('mapcol', 'sect'))
Inputs may be any that keep to these rules, and one draw needn't show every extreme that they name: `footprint_device`: among the 512 footprint blocks of one tile at most 8 name the same radar device; some tile reaches 8.
All inputs are finite; a program needn't handle non-finite values. No bound on the sum of `layover` on one device may be relied on, other than what follows from the above.
Results may differ from a plain program's by a relative error of at most 0.000068.
Values sent between devices are 32-bit elements; how exact they have to be, the bound alone decides.
A program may use at most 64 MiB of HBM per device.

v0:
```python
import math

import jax
import jax.numpy as jnp
from jax import lax
from jax.sharding import PartitionSpec as P

BR = 16
BC = 16
PIX = 128


cell_spacing = 10.0
heading_angle = 0.2


def extended(cells, sides, width):
    for axis, dim in sides:
        count = lax.axis_size(axis)
        ends = count - 1
        head = lax.slice_in_dim(cells, 0, width, axis=dim)
        tail = lax.slice_in_dim(cells, cells.shape[dim] - width, cells.shape[dim], axis=dim)
        cells = jnp.concatenate(
            [
                lax.ppermute(tail, axis, [(i, (i + 1) % count) for i in range(ends)]),
                cells,
                lax.ppermute(head, axis, [((i + 1) % count, i) for i in range(ends)]),
            ],
            axis=dim,
        )
    return cells


def pixel_table(pixels):
    return (pixels[:, :, None] == jnp.arange(PIX, dtype=jnp.int32)[None, None, :]).astype(
        jnp.float32
    )


def block_sums(pair):
    area_part, pixel_part = pair
    return jnp.einsum(
        "bc,bcp->bp", area_part, pixel_table(pixel_part), precision=lax.Precision.HIGHEST
    )


def cell_values(pair):
    value_part, pixel_part = pair
    return jnp.einsum(
        "bp,bcp->bc", value_part, pixel_table(pixel_part), precision=lax.Precision.HIGHEST
    )


def per_device(elevation, layover, footprint_pixel, footprint_device, local_block, backscatter):
    rows_tile, cols_tile = elevation.shape
    blocks_down = rows_tile // BR
    blocks_across = cols_tile // BC
    blocks_tile = blocks_down * blocks_across
    cells_block = BR * BC
    group_size = math.gcd(blocks_tile, 64)
    group_count = blocks_tile // group_size
    radar_local = backscatter.shape[0]
    rows_group = lax.axis_size("maprow")
    cols_group = lax.axis_size("mapcol")
    groups = rows_group * cols_group
    capacity = max(2, 2 * blocks_tile // groups)
    padded = extended(elevation, (("maprow", 0), (("mapcol", "sect"), 1)), 1)
    slope_cols = (padded[1:-1, 2:] - padded[1:-1, :-2]) / (2.0 * cell_spacing)
    slope_rows = (padded[2:, 1:-1] - padded[:-2, 1:-1]) / (2.0 * cell_spacing)
    total_cols = cols_tile * lax.axis_size(("mapcol", "sect"))
    column = (lax.axis_index(("mapcol", "sect")) * cols_tile + jnp.arange(cols_tile)).astype(
        jnp.float32
    )
    incidence = 0.52 + 0.28 * (column + 0.5) / total_cols
    look_cols = -jnp.sin(incidence) * jnp.cos(heading_angle)
    look_rows = -jnp.sin(incidence) * jnp.sin(heading_angle)
    look_up = jnp.cos(incidence)
    facing = -slope_cols * look_cols[None, :] - slope_rows * look_rows[None, :] + look_up[None, :]
    areas = jnp.maximum(facing, 0.0) * (1 - layover).astype(jnp.float32)

    def blockify(field):
        shaped = field.reshape(blocks_down, BR, blocks_across, BC).transpose(0, 2, 1, 3)
        return shaped.reshape(group_count, group_size, cells_block)

    area_cells = blockify(areas)
    pixel_cells = blockify(footprint_pixel)
    block_area = lax.map(block_sums, (area_cells, pixel_cells)).reshape(blocks_tile, PIX)
    target = footprint_device[0, :, 0]
    onehot = (target[:, None] == jnp.arange(groups, dtype=jnp.int32)[None, :]).astype(jnp.int32)
    running = jnp.cumsum(onehot, axis=0) - 1
    ranked = jnp.sum(onehot * running, axis=1)
    slot_index = target * capacity + ranked
    send_area = jnp.zeros((groups * capacity, PIX), jnp.float32).at[slot_index].set(block_area)
    send_ids = jnp.full((groups * capacity,), float(radar_local), jnp.float32)
    send_ids = send_ids.at[slot_index].set(local_block[0].astype(jnp.float32))
    recv_area, recv_ids = (
        lax.all_to_all(
            send_area.reshape(groups, capacity, PIX),
            ("maprow", "mapcol"),
            split_axis=0,
            concat_axis=0,
            tiled=True,
        ),
        lax.all_to_all(
            send_ids.reshape(groups, capacity),
            ("maprow", "mapcol"),
            split_axis=0,
            concat_axis=0,
            tiled=True,
        ),
    )
    recv_area = recv_area.reshape(groups * capacity, PIX)
    recv_index = recv_ids.reshape(groups * capacity).astype(jnp.int32)
    owner_table = (recv_index[:, None] == jnp.arange(radar_local, dtype=jnp.int32)[None, :]).astype(
        jnp.float32
    )
    area_sum = jnp.dot(
        owner_table.T,
        recv_area,
        precision=lax.Precision.HIGHEST,
        preferred_element_type=jnp.float32,
    )
    gamma_radar = backscatter / jnp.maximum(area_sum, 1.0)
    back_rows = jnp.dot(
        owner_table,
        gamma_radar,
        precision=lax.Precision.HIGHEST,
        preferred_element_type=jnp.float32,
    )
    returned = lax.all_to_all(
        back_rows.reshape(groups, capacity, PIX),
        ("maprow", "mapcol"),
        split_axis=0,
        concat_axis=0,
        tiled=True,
    )
    returned = returned.reshape(groups * capacity, PIX)[slot_index]
    returned = returned.reshape(group_count, group_size, PIX)
    gamma_cells = lax.map(cell_values, (returned, pixel_cells))
    gamma_map = (
        gamma_cells.reshape(blocks_down, blocks_across, BR, BC)
        .transpose(0, 2, 1, 3)
        .reshape(rows_tile, cols_tile)
    )
    return (gamma_radar, gamma_map)


def solution(mesh):
    in_specs = (
        P("maprow", ("mapcol", "sect")),
        P("maprow", ("mapcol", "sect")),
        P("maprow", ("mapcol", "sect")),
        P(("maprow", "mapcol", "sect"), None, None),
        P(("maprow", "mapcol", "sect"), None),
        P(("maprow", "mapcol", "sect"), None),
    )
    out_specs = (P(("maprow", "mapcol", "sect"), None), P("maprow", ("mapcol", "sect")))
    return jax.shard_map(
        per_device, mesh=mesh, in_specs=in_specs, out_specs=out_specs, check_vma=False
    )
```

profile of v0, /device:TPU:32, one launch (start us, length us, event | category | flops | bytes accessed | tf_op | source)
XLA Modules:
  0.0 230.4 jit_solution(17978614295821669763)
XLA Ops:
  12.7 16.1 %all-to-all-start = ((f32[128,1,8]{2,1,0:T(1,128)}), f32[128,1,8]{2,1,0:T(1,128)S(1)}, u32[]{:S(2)}, u32[]{:S(2)}) async-start(f32[128,1,8]{2,1,0:T(1,128)} %bitcast.21), calls=%async_computation | async-start | bytes 131072 | tf_op jit(solution)/shard_map/all_to_all | solution.py:104
  52.1 49.9 %while.20 = (s32[]{:T(128)}, f32[8,64,128]{2,1,0:T(8,128)}, f32[8,64,256]{2,1,0:T(8,128)S(1)}, s32[8,64,256]{2,1,0:T(8,128)}, s32[]{:T(128)}) while((s32[]{:T(128)}, f32[8,64,128]{2,1,0:T(8,128)}, f32[8,64,256]{2,1,0:T(8,128)S(1)}, s32[8,64,256]{2,1,0:T(8,128)}, s32[]{:T(128)}) %tuple.42), condition=%wide.region_5.6_spmd, body=%wide.region_4.5_spmd.sunk | while | flops 27262976 | bytes 492101 | solution.py:87
  53.0 4.8 %fusion.38 = f32[64,1,128]{2,1,0:T(1,128)S(1)} fusion(s32[64,256]{1,0:T(8,128)S(1)} %dynamic-slice_bitcast_fusion.6, f32[64,256,1]{1,0,2:T(8,128)S(1)} %dynamic-slice_bitcast_fusion.7), kind=kOutput, calls=%fused_computation.4.clone.1 | convolution fusion | flops 27262976 | bytes 163840 | tf_op jit(solution)/shard_map/while/body/eval_jaxpr/bc,bcp->bp/dot_general | solution.py:42
  59.2 4.8 %fusion.38 = f32[64,1,128]{2,1,0:T(1,128)S(1)} fusion(s32[64,256]{1,0:T(8,128)S(1)} %dynamic-slice_bitcast_fusion.6, f32[64,256,1]{1,0,2:T(8,128)S(1)} %dynamic-slice_bitcast_fusion.7), kind=kOutput, calls=%fused_computation.4.clone.1 | convolution fusion | flops 27262976 | bytes 163840 | tf_op jit(solution)/shard_map/while/body/eval_jaxpr/bc,bcp->bp/dot_general | solution.py:42
  65.5 4.8 %fusion.38 = f32[64,1,128]{2,1,0:T(1,128)S(1)} fusion(s32[64,256]{1,0:T(8,128)S(1)} %dynamic-slice_bitcast_fusion.6, f32[64,256,1]{1,0,2:T(8,128)S(1)} %dynamic-slice_bitcast_fusion.7), kind=kOutput, calls=%fused_computation.4.clone.1 | convolution fusion | flops 27262976 | bytes 163840 | tf_op jit(solution)/shard_map/while/body/eval_jaxpr/bc,bcp->bp/dot_general | solution.py:42
  71.7 4.8 %fusion.38 = f32[64,1,128]{2,1,0:T(1,128)S(1)} fusion(s32[64,256]{1,0:T(8,128)S(1)} %dynamic-slice_bitcast_fusion.6, f32[64,256,1]{1,0,2:T(8,128)S(1)} %dynamic-slice_bitcast_fusion.7), kind=kOutput, calls=%fused_computation.4.clone.1 | convolution fusion | flops 27262976 | bytes 163840 | tf_op jit(solution)/shard_map/while/body/eval_jaxpr/bc,bcp->bp/dot_general | solution.py:42
  77.9 4.8 %fusion.38 = f32[64,1,128]{2,1,0:T(1,128)S(1)} fusion(s32[64,256]{1,0:T(8,128)S(1)} %dynamic-slice_bitcast_fusion.6, f32[64,256,1]{1,0,2:T(8,128)S(1)} %dynamic-slice_bitcast_fusion.7), kind=kOutput, calls=%fused_computation.4.clone.1 | convolution fusion | flops 27262976 | bytes 163840 | tf_op jit(solution)/shard_map/while/body/eval_jaxpr/bc,bcp->bp/dot_general | solution.py:42
  84.1 4.8 %fusion.38 = f32[64,1,128]{2,1,0:T(1,128)S(1)} fusion(s32[64,256]{1,0:T(8,128)S(1)} %dynamic-slice_bitcast_fusion.6, f32[64,256,1]{1,0,2:T(8,128)S(1)} %dynamic-slice_bitcast_fusion.7), kind=kOutput, calls=%fused_computation.4.clone.1 | convolution fusion | flops 27262976 | bytes 163840 | tf_op jit(solution)/shard_map/while/body/eval_jaxpr/bc,bcp->bp/dot_general | solution.py:42
  90.4 4.8 %fusion.38 = f32[64,1,128]{2,1,0:T(1,128)S(1)} fusion(s32[64,256]{1,0:T(8,128)S(1)} %dynamic-slice_bitcast_fusion.6, f32[64,256,1]{1,0,2:T(8,128)S(1)} %dynamic-slice_bitcast_fusion.7), kind=kOutput, calls=%fused_computation.4.clone.1 | convolution fusion | flops 27262976 | bytes 163840 | tf_op jit(solution)/shard_map/while/body/eval_jaxpr/bc,bcp->bp/dot_general | solution.py:42
  96.6 4.8 %fusion.38 = f32[64,1,128]{2,1,0:T(1,128)S(1)} fusion(s32[64,256]{1,0:T(8,128)S(1)} %dynamic-slice_bitcast_fusion.6, f32[64,256,1]{1,0,2:T(8,128)S(1)} %dynamic-slice_bitcast_fusion.7), kind=kOutput, calls=%fused_computation.4.clone.1 | convolution fusion | flops 27262976 | bytes 163840 | tf_op jit(solution)/shard_map/while/body/eval_jaxpr/bc,bcp->bp/dot_general | solution.py:42
  104.8 13.8 %all-to-all-start.1 = ((f32[128,8,128]{2,1,0:T(8,128)}), f32[128,8,128]{2,1,0:T(8,128)S(1)}, u32[]{:S(2)}, u32[]{:S(2)}) async-start(f32[128,8,128]{2,1,0:T(8,128)} %bitcast.25), calls=%async_computation.1 | async-start | bytes 1048576 | tf_op jit(solution)/shard_map/all_to_all | solution.py:97
  118.9 20.2 %all-to-all-done.1 = f32[128,8,128]{2,1,0:T(8,128)S(1)} async-done(((f32[128,8,128]{2,1,0:T(8,128)}), f32[128,8,128]{2,1,0:T(8,128)S(1)}, u32[]{:S(2)}, u32[]{:S(2)}) %all-to-all-start.1) | async-done | bytes 524320 | tf_op jit(solution)/shard_map/all_to_all | solution.py:97
  141.1 6.6 %all-to-all-start.2 = ((f32[128,8,128]{2,1,0:T(8,128)}), f32[128,8,128]{2,1,0:T(8,128)S(1)}, u32[]{:S(2)}, u32[]{:S(2)}) async-start(f32[128,8,128]{2,1,0:T(8,128)} %convolution_bitcast_fusion), calls=%async_computation.2 | async-start | bytes 1048576 | tf_op jit(solution)/shard_map/all_to_all | solution.py:130
  147.8 19.1 %all-to-all-done.2 = f32[128,8,128]{2,1,0:T(8,128)S(1)} async-done(((f32[128,8,128]{2,1,0:T(8,128)}), f32[128,8,128]{2,1,0:T(8,128)S(1)}, u32[]{:S(2)}, u32[]{:S(2)}) %all-to-all-start.2) | async-done | bytes 524320 | tf_op jit(solution)/shard_map/all_to_all | solution.py:130
  167.9 53.8 %while.21 = (s32[]{:T(128)}, f32[8,64,256]{2,1,0:T(8,128)S(1)}, f32[8,64,128]{2,1,0:T(8,128)S(1)}, s32[8,64,256]{2,1,0:T(8,128)}, s32[]{:T(128)}) while((s32[]{:T(128)}, f32[8,64,256]{2,1,0:T(8,128)S(1)}, f32[8,64,128]{2,1,0:T(8,128)S(1)}, s32[8,64,256]{2,1,0:T(8,128)}, s32[]{:T(128)}) %tuple.49), condition=%wide.region_8.9_spmd, body=%wide.region_7.8_spmd.sunk | while | flops 27262976 | bytes 491593 | solution.py:139
  168.8 5.8 %fusion.40 = f32[64,1,256]{2,1,0:T(1,128)S(1)} fusion(f32[64,128,1]{1,2,0:T(1,128)S(1)} %bitcast.82, s32[64,256]{1,0:T(8,128)S(1)} %dynamic-slice_bitcast_fusion.8), kind=kOutput, calls=%fused_computation.11.clone.1 | convolution fusion | flops 27262976 | bytes 163840 | tf_op jit(solution)/shard_map/while/body/eval_jaxpr/bp,bcp->bc/dot_general | solution.py:49
  175.5 5.8 %fusion.40 = f32[64,1,256]{2,1,0:T(1,128)S(1)} fusion(f32[64,128,1]{1,2,0:T(1,128)S(1)} %bitcast.82, s32[64,256]{1,0:T(8,128)S(1)} %dynamic-slice_bitcast_fusion.8), kind=kOutput, calls=%fused_computation.11.clone.1 | convolution fusion | flops 27262976 | bytes 163840 | tf_op jit(solution)/shard_map/while/body/eval_jaxpr/bp,bcp->bc/dot_general | solution.py:49
  182.2 5.8 %fusion.40 = f32[64,1,256]{2,1,0:T(1,128)S(1)} fusion(f32[64,128,1]{1,2,0:T(1,128)S(1)} %bitcast.82, s32[64,256]{1,0:T(8,128)S(1)} %dynamic-slice_bitcast_fusion.8), kind=kOutput, calls=%fused_computation.11.clone.1 | convolution fusion | flops 27262976 | bytes 163840 | tf_op jit(solution)/shard_map/while/body/eval_jaxpr/bp,bcp->bc/dot_general | solution.py:49
  189.0 5.8 %fusion.40 = f32[64,1,256]{2,1,0:T(1,128)S(1)} fusion(f32[64,128,1]{1,2,0:T(1,128)S(1)} %bitcast.82, s32[64,256]{1,0:T(8,128)S(1)} %dynamic-slice_bitcast_fusion.8), kind=kOutput, calls=%fused_computation.11.clone.1 | convolution fusion | flops 27262976 | bytes 163840 | tf_op jit(solution)/shard_map/while/body/eval_jaxpr/bp,bcp->bc/dot_general | solution.py:49
  195.7 5.8 %fusion.40 = f32[64,1,256]{2,1,0:T(1,128)S(1)} fusion(f32[64,128,1]{1,2,0:T(1,128)S(1)} %bitcast.82, s32[64,256]{1,0:T(8,128)S(1)} %dynamic-slice_bitcast_fusion.8), kind=kOutput, calls=%fused_computation.11.clone.1 | convolution fusion | flops 27262976 | bytes 163840 | tf_op jit(solution)/shard_map/while/body/eval_jaxpr/bp,bcp->bc/dot_general | solution.py:49
  202.4 5.8 %fusion.40 = f32[64,1,256]{2,1,0:T(1,128)S(1)} fusion(f32[64,128,1]{1,2,0:T(1,128)S(1)} %bitcast.82, s32[64,256]{1,0:T(8,128)S(1)} %dynamic-slice_bitcast_fusion.8), kind=kOutput, calls=%fused_computation.11.clone.1 | convolution fusion | flops 27262976 | bytes 163840 | tf_op jit(solution)/shard_map/while/body/eval_jaxpr/bp,bcp->bc/dot_general | solution.py:49
  209.1 5.8 %fusion.40 = f32[64,1,256]{2,1,0:T(1,128)S(1)} fusion(f32[64,128,1]{1,2,0:T(1,128)S(1)} %bitcast.82, s32[64,256]{1,0:T(8,128)S(1)} %dynamic-slice_bitcast_fusion.8), kind=kOutput, calls=%fused_computation.11.clone.1 | convolution fusion | flops 27262976 | bytes 163840 | tf_op jit(solution)/shard_map/while/body/eval_jaxpr/bp,bcp->bc/dot_general | solution.py:49
  215.9 5.8 %fusion.40 = f32[64,1,256]{2,1,0:T(1,128)S(1)} fusion(f32[64,128,1]{1,2,0:T(1,128)S(1)} %bitcast.82, s32[64,256]{1,0:T(8,128)S(1)} %dynamic-slice_bitcast_fusion.8), kind=kOutput, calls=%fused_computation.11.clone.1 | convolution fusion | flops 27262976 | bytes 163840 | tf_op jit(solution)/shard_map/while/body/eval_jaxpr/bp,bcp->bc/dot_general | solution.py:49
  225.3 5.1 %reshape.133 = f32[256,512]{1,0:T(8,128)} reshape(f32[16,16,32,16]{3,2,1,0:T(8,128)} %copy.30) | data formatting | bytes 1048576 | tf_op jit(solution)/shard_map/reshape | solution.py:143
  (98 shorter events, 63.6 us)
Async XLA Ops:
  1.4 27.5 %collective-permute-start = (f32[1,512]{1,0:T(1,128)S(1)}, f32[1,512]{1,0:T(1,128)S(1)}, u32[]{:S(2)}, u32[]{:S(2)}) collective-permute-start(f32[1,512]{1,0:T(1,128)S(1)} %get-tuple-element.83), channel_id=1, source_target_pairs={{0,16},{16,32},{32,48},{48,64},{64,80},{80,96},{96,112},{112,128},... | collective-permute-start | bytes 6152 | tf_op jit(solution)/shard_map/ppermute | solution.py:25
  4.8 24.0 %collective-permute-start.1 = (f32[1,512]{1,0:T(1,128)S(1)}, f32[1,512]{1,0:T(1,128)S(1)}, u32[]{:S(2)}, u32[]{:S(2)}) collective-permute-start(f32[1,512]{1,0:T(1,128)S(1)} %get-tuple-element.82), channel_id=1, source_target_pairs={{16,0},{32,16},{48,32},{64,48},{80,64},{96,80},{112,96},{128,112},... | collective-permute-start | bytes 6152 | tf_op jit(solution)/shard_map/ppermute | solution.py:27
  12.7 92.1 %all-to-all-start = ((f32[128,1,8]{2,1,0:T(1,128)}), f32[128,1,8]{2,1,0:T(1,128)S(1)}, u32[]{:S(2)}, u32[]{:S(2)}) async-start(f32[128,1,8]{2,1,0:T(1,128)} %bitcast.21), calls=%async_computation | async-start | bytes 131072 | tf_op jit(solution)/shard_map/all_to_all | solution.py:104
  30.6 12.6 %collective-permute-start.2 = (f32[258,1]{1,0:T(8,128)}, f32[258,1]{1,0:T(8,128)S(1)}, u32[]{:S(2)}, u32[]{:S(2)}) collective-permute-start(f32[258,1]{1,0:T(8,128)} %get-tuple-element.80), channel_id=1, source_target_pairs={{1,0},{2,1},{3,2},{4,3},{5,4},{6,5},{7,6},{8,7},{9,8},{10,9},{11,1... | collective-permute-start | bytes 3104 | tf_op jit(solution)/shard_map/ppermute | solution.py:27
  32.6 10.7 %collective-permute-start.3 = (f32[258,1]{1,0:T(8,128)}, f32[258,1]{1,0:T(8,128)S(1)}, u32[]{:S(2)}, u32[]{:S(2)}) collective-permute-start(f32[258,1]{1,0:T(8,128)} %get-tuple-element.81), channel_id=1, source_target_pairs={{0,1},{1,2},{2,3},{3,4},{4,5},{5,6},{6,7},{7,8},{8,9},{9,10},{10,1... | collective-permute-start | bytes 3104 | tf_op jit(solution)/shard_map/ppermute | solution.py:25
  52.1 87.0 %copy-start.1 = (f32[128,128]{1,0:T(8,128)S(1)}, f32[128,128]{1,0:T(8,128)}, u32[]{:S(2)}) copy-start(f32[128,128]{1,0:T(8,128)} %param.15) | copy-start | bytes 196612
  104.8 34.3 %all-to-all-start.1 = ((f32[128,8,128]{2,1,0:T(8,128)}), f32[128,8,128]{2,1,0:T(8,128)S(1)}, u32[]{:S(2)}, u32[]{:S(2)}) async-start(f32[128,8,128]{2,1,0:T(8,128)} %bitcast.25), calls=%async_computation.1 | async-start | bytes 1048576 | tf_op jit(solution)/shard_map/all_to_all | solution.py:97
  139.9 28.0 %copy-start = (f32[128,128]{1,0:T(8,128)}, f32[128,128]{1,0:T(8,128)S(1)}, u32[]{:S(2)}) copy-start(f32[128,128]{1,0:T(8,128)S(1)} %fusion.5) | copy-start | bytes 196612
  141.1 25.7 %all-to-all-start.2 = ((f32[128,8,128]{2,1,0:T(8,128)}), f32[128,8,128]{2,1,0:T(8,128)S(1)}, u32[]{:S(2)}, u32[]{:S(2)}) async-start(f32[128,8,128]{2,1,0:T(8,128)} %convolution_bitcast_fusion), calls=%async_computation.2 | async-start | bytes 1048576 | tf_op jit(solution)/shard_map/all_to_all | solution.py:130
where the time goes:
time: 232 us; the launch traced here: 230 us
  matrix products  86.7 us (37%)
  local copies, waits for them, and re-layouts  50.7 us (22%)
  starting transfers between devices  45.6 us (20%)
  waiting for transfers between devices  39.3 us (17%)
  other arithmetic  6.99 us (3%)
    dot_general x8, matrix products, cell_values(): jnp.einsum('bp,bcp->bc', value_part, pixel_table(pixel_part), precision=l...  46.7 us
    dot_general x8, matrix products, block_sums(): jnp.einsum('bc,bcp->bp', area_part, pixel_table(pixel_part), precision=la...  38 us
    all_to_all x1, waiting for transfers between devices, per_device(): lax.all_to_all(send_area.reshape(groups, capacity, PIX), ('maprow', 'mapc...  20.2 us
    all_to_all x1, waiting for transfers between devices, per_device(): lax.all_to_all(back_rows.reshape(groups, capacity, PIX), ('maprow', 'mapc...  19.1 us
    all_to_all x1, starting transfers between devices, per_device(): lax.all_to_all(send_ids.reshape(groups, capacity), ('maprow', 'mapcol'),...  16.1 us
    all_to_all x1, starting transfers between devices, per_device(): lax.all_to_all(send_area.reshape(groups, capacity, PIX), ('maprow', 'mapc...  13.8 us
    eq x16, local copies, waits for them, and re-layouts, pixel_table(): pixels[:, :, None] == jnp.arange(PIX, dtype=jnp.int32)[None, None, :]  13.6 us
    all_to_all x1, starting transfers between devices, per_device(): lax.all_to_all(back_rows.reshape(groups, capacity, PIX), ('maprow', 'mapc...  6.61 us
  transfers between devices with their start and end apart: 7, of which 2 were waited for; matrix products, arithmetic and copies ran while one was open for 34% of the time, Pallas kernels for 0%

commit v1 on v0

v1 whole, which is shorter than its diff:
```python
import functools

import jax
import jax.numpy as jnp
from jax import lax
from jax.experimental import pallas as pl
from jax.experimental.pallas import tpu as pltpu
from jax.sharding import PartitionSpec as P

BR = 16
BC = 16
PIX = 128
CELL_SPACING = 10.0
HEADING = 0.2
MESH = pl.DeviceIdType.MESH
F32 = jnp.float32
BF16 = jnp.bfloat16


def iota(shape, dim):
    return lax.broadcasted_iota(jnp.int32, shape, dim)


def iotaf(shape, dim):
    return iota(shape, dim).astype(F32)


def swap_groups(x):
    lane, row = iota((8, 128), 1), iota((8, 128), 0)
    x = pltpu.roll(x, 0, 1, stride=16, stride_axis=0)
    x = jnp.take_along_axis(x, ((lane >> 4) - row) & 7, axis=0)
    return jnp.take_along_axis(x, (lane + 16 * row) & 127, axis=1)


def split(x):
    first = x.astype(BF16)
    return jnp.concatenate([first, (x - first.astype(F32)).astype(BF16)], axis=1)


def folded(x):
    half = x.shape[1] // 2
    return x[:, :half] + x[:, half:]


def dot(a, b):
    return lax.dot_general(a, b, (((1,), (0,)), ((), ())), preferred_element_type=F32)


def dot_nt(a, b):
    return lax.dot_general(a, b, (((1,), (1,)), ((), ())), preferred_element_type=F32)


def block_sums(area, pixel):
    firsts, seconds, lows = [], [], []
    for half in range(2):
        a = swap_groups(area[8 * half : 8 * half + 8])
        p = swap_groups(pixel[8 * half : 8 * half + 8])
        a1 = a.astype(BF16).astype(F32)
        a2 = a - a1
        is_high = (p >> 4)[:, None, :] == iota((8, 8, 128), 1)
        is_low = (p & 15)[:, None, :] == iota((8, 16, 128), 1)
        firsts.append(jnp.where(is_high, a1[:, None, :], 0.0).reshape(64, 128))
        seconds.append(jnp.where(is_high, a2[:, None, :], 0.0).reshape(64, 128))
        lows.append(jnp.where(is_low, 1.0, 0.0).reshape(128, 128))
    left = jnp.concatenate(
        [jnp.concatenate(firsts, axis=1), jnp.concatenate(seconds, axis=1)], axis=0
    ).astype(BF16)
    right = jnp.concatenate(lows, axis=1).astype(BF16)
    out = dot_nt(left, right)
    out = out[:64] + out[64:]
    group = iota((8, 128), 1) >> 4
    own = out[0:8]
    for b in range(1, 8):
        own = jnp.where(group == b, out[8 * b : 8 * b + 8], own)
    return swap_groups(own)


def exchange(
    nr, nz, cap,
    elev, lay, pix, target, local, back,
    gamma, found,
    epad, layv, pixv, look, pmat, pmt, oht, oh, hist, sendb, recvb, idsend, idrecv,
    dense, cin, gin, backb, retb,
    in_sem, halo_send, halo_recv, id_send, id_recv, out_send, out_recv,
    chain_send, chain_recv, gchain_send, gchain_recv, ret_send, ret_recv,
):
    rows, cols = elev.shape
    tb = target.shape[1]
    dests = nr * nz
    h = nz // 2
    tiles = cols // 128
    r, c, s = lax.axis_index("maprow"), lax.axis_index("mapcol"), lax.axis_index("sect")
    up_z, down_z = {"mapcol": lax.rem(c + 1, nz)}, {"mapcol": lax.rem(c + nz - 1, nz)}
    west = {"mapcol": lax.rem(c + nz - 1 + s, nz), "sect": 1 - s}
    east = {"mapcol": lax.rem(c + s, nz), "sect": 1 - s}
    north, south = {"maprow": lax.rem(r + nr - 1, nr)}, {"maprow": lax.rem(r + 1, nr)}
    spans = [(0, 1)] + [(2 * g - 1, 2 * g + 1) for g in range(1, h)] + [(nz - 1, nz)]

    def place(k):
        return 2 * (k - h) if k >= h else 2 * (h - k) - 1

    barrier = pltpu.get_barrier_semaphore()

    def greet(j, carry):
        pl.semaphore_signal(
            barrier, inc=1, device_id={"maprow": lax.rem(r + j, nr)}, device_id_type=MESH
        )
        return carry

    lax.fori_loop(1, nr, greet, 0)
    for neighbour in (up_z, down_z, west, east):
        pl.semaphore_signal(barrier, inc=1, device_id=neighbour, device_id_type=MESH)

    loads = [
        pltpu.make_async_copy(elev, epad.at[8 : 8 + rows, 128 : 128 + cols], in_sem.at[0]),
        pltpu.make_async_copy(lay, layv, in_sem.at[1]),
        pltpu.make_async_copy(pix, pixv, in_sem.at[2]),
    ]
    for load in loads:
        load.start()

    name = target[...]
    step_z = ((name & (nz - 1)) + (nz - c)) & (nz - 1)
    ahead = step_z - h
    order = jnp.where(ahead >= 0, 2 * ahead, -2 * ahead - 1)
    spot = (name >> (nz.bit_length() - 1)) * nz + order
    onehot = iota((dests, tb), 0) == spot
    earlier = jnp.where(iota((tb, tb), 0) < iota((tb, tb), 1), 1.0, 0.0).astype(BF16)
    running = dot(jnp.where(onehot, 1.0, 0.0).astype(BF16), earlier)
    rank = jnp.sum(jnp.where(onehot, running, 0.0), axis=0, keepdims=True)
    slot = (spot * cap).astype(F32) + rank
    ids = jnp.where(onehot, local[...].astype(F32), 0.0).astype(BF16)
    at_lane = (r * cap).astype(F32) + rank
    lanes = jnp.where(iotaf((128, tb), 0) == at_lane, 1.0, 0.0).astype(BF16)
    idsend[...] = dot_nt(ids, lanes).reshape(nr, nz, 128)
    idrecv[pl.ds(r, 1)] = idsend[pl.ds(r, 1)]

    pl.semaphore_wait(barrier, nr - 1 + 4)

    halos = [
        (elev.at[rows - 8 : rows, :], epad.at[0:8, 128 : 128 + cols], south),
        (elev.at[0:8, :], epad.at[rows + 8 : rows + 16, 128 : 128 + cols], north),
        (elev.at[:, cols - 128 : cols], epad.at[8 : 8 + rows, 0:128], east),
        (elev.at[:, 0:128], epad.at[8 : 8 + rows, 128 + cols : 256 + cols], west),
    ]
    halos = [
        pltpu.make_async_remote_copy(
            src_ref=src, dst_ref=dst, send_sem=halo_send.at[i], recv_sem=halo_recv.at[i],
            device_id=where, device_id_type=MESH,
        )
        for i, (src, dst, where) in enumerate(halos)
    ]
    for halo in halos:
        halo.start()

    def to_plane(source, sink, send_sem, recv_sem):
        def body(j, carry):
            peer = lax.rem(r + j, nr)
            pltpu.make_async_remote_copy(
                src_ref=source(peer), dst_ref=sink(r), send_sem=send_sem, recv_sem=recv_sem,
                device_id={"maprow": peer}, device_id_type=MESH,
            ).start()
            return carry

        lax.fori_loop(1, nr, body, 0)

    def arrived(part, sem):
        pltpu.make_async_copy(part, part, sem).wait()

    to_plane(lambda i: idsend.at[i], lambda i: idrecv.at[i], id_send.at[0], id_recv.at[0])

    i0 = iota((128, 1), 0)
    row_slot = ((i0 // cap) * (nz * cap) + lax.rem(i0, cap)).astype(F32)
    i1 = iota((1, 128), 1)
    lane_slot = ((i1 // cap) * (nz * cap) + lax.rem(i1, cap)).astype(F32)
    slot_down = jnp.transpose(jnp.broadcast_to(slot, (128, tb)))
    for p in range(nz):
        pmat[p] = jnp.where(row_slot + float(p * cap) == slot, 1.0, 0.0).astype(BF16)
        pmt[:, 128 * p : 128 * p + 128] = jnp.where(
            slot_down == lane_slot + float(p * cap), 1.0, 0.0
        ).astype(BF16)

    column = ((c * 2 + s) * cols + iota((1, cols), 1)).astype(F32)
    incidence = 0.52 + 0.28 * (column + 0.5) / float(cols * nz * 2)
    sine, heading = jnp.sin(incidence), jnp.full((1, cols), HEADING, F32)
    look[0:1, :] = -sine * jnp.cos(heading) / (2.0 * CELL_SPACING)
    look[1:2, :] = -sine * jnp.sin(heading) / (2.0 * CELL_SPACING)
    look[2:3, :] = jnp.cos(incidence)

    for load in loads:
        load.wait()
    for halo in halos:
        halo.wait_recv()

    @pl.when(r == 0)
    def _():
        epad[0:8, 128 : 128 + cols] = jnp.zeros((8, cols), F32)

    @pl.when(r == nr - 1)
    def _():
        epad[rows + 8 : rows + 16, 128 : 128 + cols] = jnp.zeros((8, cols), F32)

    @pl.when((c == 0) & (s == 0))
    def _():
        epad[8 : 8 + rows, 0:128] = jnp.zeros((rows, 128), F32)

    @pl.when((c == nz - 1) & (s == 1))
    def _():
        epad[8 : 8 + rows, 128 + cols : 256 + cols] = jnp.zeros((rows, 128), F32)

    def band(i, carry):
        top = pl.multiple_of(i * BR, BR)
        lane = iota((BR, 128), 1)
        around = epad[pl.ds(top, 32), 128 : 128 + cols]
        mid = epad[pl.ds(pl.multiple_of(top + 8, 8), BR), :]
        mids = [mid[:, 128 * j : 128 * j + 128] for j in range(tiles + 2)]
        right = [pltpu.roll(x, 1, 1) for x in mids[:-1]]
        left = [pltpu.roll(x, 127, 1) for x in mids[1:]]
        for j in range(tiles):
            at = slice(128 * j, 128 * j + 128)
            before = jnp.where(lane == 0, right[j], right[j + 1])
            after = jnp.where(lane == 127, left[j + 1], left[j])
            rise_cols = after - before
            rise_rows = around[9:25, at] - around[7:23, at]
            facing = (
                look[2:3, at] - rise_cols * look[0:1, at] - rise_rows * look[1:2, at]
            )
            lit = (1 - layv[pl.ds(top, BR), at]).astype(F32)
            area = jnp.maximum(facing, 0.0) * lit
            sums = block_sums(area, pixv[pl.ds(top, BR), at])
            hist[pl.ds(pl.multiple_of(i * (tiles * 8) + 8 * j, 8), 8), :] = sums
        return carry

    lax.fori_loop(0, rows // BR, band, 0)

    terms = split(hist[...])
    for g, (p0, p1) in enumerate(spans):
        for p in range(p0, p1):
            sendb[:, p] = folded(dot(pmat[p], terms)).reshape(nr, cap, PIX)
        recvb[pl.ds(r, 1), p0:p1] = sendb[pl.ds(r, 1), p0:p1]
        to_plane(
            lambda i: sendb.at[i, p0:p1], lambda i: recvb.at[i, p0:p1],
            out_send.at[g], out_recv.at[g],
        )

    arrived(idrecv.at[0 : nr - 1], id_recv.at[0])
    names = idrecv[0]
    for i in range(1, nr):
        names = names + idrecv[i]
    for p in range(nz):
        wide = jnp.broadcast_to(names[p : p + 1, :], (128, 128))
        oht[p] = jnp.where(wide == iotaf((128, 128), 0), 1.0, 0.0).astype(BF16)
        oh[p] = jnp.where(jnp.transpose(wide) == iotaf((128, 128), 1), 1.0, 0.0).astype(BF16)

    def hop(source, sinks, sends, recvs, way, j, q):
        return pltpu.make_async_remote_copy(
            src_ref=source, dst_ref=sinks.at[way, j, q],
            send_sem=sends.at[way, j, q], recv_sem=recvs.at[way, j, q],
            device_id=(up_z, down_z)[way], device_id_type=MESH,
        )

    def pieces(j, last):
        if j == last:
            return [(0, 0), (1, 1)]
        return [(w, q) for q in range(2) for w in range(2)]

    hops = {}
    for g, (p0, p1) in enumerate(spans):
        arrived(recvb.at[0 : nr - 1, p0:p1], out_recv.at[g])
        for p in range(p0, p1):
            dense[p] = folded(dot(oht[p], split(recvb[:, p].reshape(128, PIX))))
        if g < h:
            for way, q in pieces(g + 1, 1):
                p = place(h - g if way == 0 else h + g)
                part = slice(64 * q, 64 * q + 64)
                if (way, g, q) in hops:
                    hops[way, g, q].wait_recv()
                    dense[p, part] = dense[p, part] + cin[way, g, q]
                hops[way, g + 1, q] = hop(
                    dense.at[p, part], cin, chain_send, chain_recv, way, g + 1, q
                )
                hops[way, g + 1, q].start()
        else:
            for q in range(2):
                part = slice(64 * q, 64 * q + 64)
                total = dense[p0, part]
                for way in range(2):
                    if (way, g, q) in hops:
                        hops[way, g, q].wait_recv()
                        total = total + cin[way, g, q]
                gamma[part] = back[part] / jnp.maximum(total, 1.0)

    ghops = {}

    def pass_on(j):
        for way, q in pieces(j, h):
            source = gamma.at[64 * q : 64 * q + 64] if j == 1 else gin.at[way, j - 1, q]
            if j > 1:
                ghops[way, j - 1, q].wait_recv()
            ghops[way, j, q] = hop(source, gin, gchain_send, gchain_recv, way, j, q)
            ghops[way, j, q].start()

    def give(g, tables):
        p0, p1 = spans[g]
        for p, table in zip(range(p0, p1), tables):
            backb[:, p] = folded(dot(oh[p], split(table))).reshape(nr, cap, PIX)
        retb[pl.ds(r, 1), p0:p1] = backb[pl.ds(r, 1), p0:p1]
        to_plane(
            lambda i: backb.at[i, p0:p1], lambda i: retb.at[i, p0:p1],
            ret_send.at[g], ret_recv.at[g],
        )

    def take(g):
        p0, p1 = spans[g]
        arrived(retb.at[0 : nr - 1, p0:p1], ret_recv.at[g])
        given = jnp.concatenate(
            [split(retb[:, p].reshape(128, PIX)) for p in range(p0, p1)], axis=0
        )
        rows_found = folded(dot(pmt[:, 128 * p0 : 128 * p1], given))
        found[...] = rows_found if g == h else found[...] + rows_found

    pass_on(1)
    give(h, [gamma[...]])
    for j in range(1, h):
        pass_on(j + 1)
        for way, q in pieces(j, h):
            if (way, j + 1, q) not in ghops:
                ghops[way, j, q].wait_recv()
        give(h - j, [gin[1, j].reshape(128, PIX), gin[0, j].reshape(128, PIX)])
        take(h - j + 1)
    for way, q in pieces(h, h):
        ghops[way, h, q].wait_recv()
    give(0, [jnp.concatenate([gin[0, h, 0], gin[1, h, 1]], axis=0)])
    if h > 1:
        take(1)
    take(0)

    for halo in halos:
        halo.wait_send()
    arrived(idsend.at[0 : nr - 1], id_send.at[0])
    for g, (p0, p1) in enumerate(spans):
        arrived(sendb.at[0 : nr - 1, p0:p1], out_send.at[g])
        arrived(backb.at[0 : nr - 1, p0:p1], ret_send.at[g])
    for one in (*hops.values(), *ghops.values()):
        one.wait_send()


def lookup(bands, found, pix, out):
    tiles = out.shape[1] // 128

    def band(i, carry):
        for j in range(tiles):
            at = slice(128 * j, 128 * j + 128)
            table = found[pl.ds(pl.multiple_of(i * (tiles * 8) + 8 * j, 8), 8), :]
            for half in range(2):
                span = pl.ds(pl.multiple_of(i * BR + 8 * half, 8), 8)
                place = swap_groups(pix[span, at])
                out[span, at] = swap_groups(jnp.take_along_axis(table, place, axis=1))
        return carry

    lax.fori_loop(0, bands, band, 0)


def per_device(nr, nz, elevation, layover, footprint_pixel, footprint_device, local_block, backscatter):
    rows, cols = elevation.shape
    tb = local_block.shape[1]
    cap = max(2, 2 * tb // (nr * nz))
    h = nz // 2
    held = backscatter.shape[0]
    vmem = pl.BlockSpec(memory_space=pltpu.VMEM)
    hbm = pl.BlockSpec(memory_space=pl.ANY)
    dma = pltpu.SemaphoreType.DMA
    gamma, found = pl.pallas_call(
        functools.partial(exchange, nr, nz, cap),
        out_shape=(
            jax.ShapeDtypeStruct((held, PIX), F32),
            jax.ShapeDtypeStruct((tb, PIX), F32),
        ),
        in_specs=[hbm, hbm, hbm, vmem, vmem, vmem],
        out_specs=(vmem, vmem),
        scratch_shapes=[
            pltpu.VMEM((rows + 16, cols + 256), F32),
            pltpu.VMEM((rows, cols), jnp.int32),
            pltpu.VMEM((rows, cols), jnp.int32),
            pltpu.VMEM((8, cols), F32),
            pltpu.VMEM((nz, 128, tb), BF16),
            pltpu.VMEM((tb, nz * 128), BF16),
            pltpu.VMEM((nz, 128, 128), BF16),
            pltpu.VMEM((nz, 128, 128), BF16),
            pltpu.VMEM((tb, PIX), F32),
            pltpu.VMEM((nr, nz, cap, PIX), F32),
            pltpu.VMEM((nr, nz, cap, PIX), F32),
            pltpu.VMEM((nr, nz, 128), F32),
            pltpu.VMEM((nr, nz, 128), F32),
            pltpu.VMEM((nz, 128, PIX), F32),
            pltpu.VMEM((2, h + 1, 2, 64, PIX), F32),
            pltpu.VMEM((2, h + 1, 2, 64, PIX), F32),
            pltpu.VMEM((nr, nz, cap, PIX), F32),
            pltpu.VMEM((nr, nz, cap, PIX), F32),
            dma((3,)),
            dma((4,)),
            dma((4,)),
            dma((1,)),
            dma((1,)),
            dma((h + 1,)),
            dma((h + 1,)),
            dma((2, h + 1, 2)),
            dma((2, h + 1, 2)),
            dma((2, h + 1, 2)),
            dma((2, h + 1, 2)),
            dma((h + 1,)),
            dma((h + 1,)),
        ],
        compiler_params=pltpu.CompilerParams(
            collective_id=0, has_side_effects=True, vmem_limit_bytes=40 * 2**20
        ),
    )(
        elevation, layover, footprint_pixel,
        footprint_device.reshape(1, tb), local_block, backscatter,
    )
    gamma_map = pl.pallas_call(
        functools.partial(lookup, rows // BR),
        out_shape=jax.ShapeDtypeStruct((rows, cols), F32),
        in_specs=[vmem, vmem],
        out_specs=vmem,
        compiler_params=pltpu.CompilerParams(vmem_limit_bytes=16 * 2**20),
    )(found, footprint_pixel)
    return gamma, gamma_map


def solution(mesh):
    in_specs = (
        P("maprow", ("mapcol", "sect")),
        P("maprow", ("mapcol", "sect")),
        P("maprow", ("mapcol", "sect")),
        P(("maprow", "mapcol", "sect"), None, None),
        P(("maprow", "mapcol", "sect"), None),
        P(("maprow", "mapcol", "sect"), None),
    )
    out_specs = (P(("maprow", "mapcol", "sect"), None), P("maprow", ("mapcol", "sect")))
    return jax.shard_map(
        functools.partial(per_device, mesh.shape["maprow"], mesh.shape["mapcol"]),
        mesh=mesh,
        in_specs=in_specs,
        out_specs=out_specs,
        check_vma=False,
    )
```

time: 232 us -> 76 us (0.33)
  matrix products: 86.7 us -> 0 us
  Pallas kernels: 0 us -> 68.3 us
  starting transfers between devices: 45.6 us -> 0 us
  local copies, waits for them, and re-layouts: 50.7 us -> 5.95 us
  waiting for transfers between devices: 39.3 us -> 0 us
  other arithmetic: 6.99 us -> 0 us
    dot_general x18 -> x0, matrix products: 86.7 us -> none  [the longest x8 46.7 us: cell_values(): jnp.einsum('bp,bcp->bc', value_part, pixel_table(pixel_part), precision=l...]
    pallas_call x0 -> x2, Pallas kernels: none -> 68.3 us  [the longest x1 61.7 us: per_device(): pl.pallas_call(functools.partial(exchange, nr, nz, cap), out_shape=(jax.S...]
    all_to_all x3 -> x0, waiting for transfers between devices: 39.3 us -> none  [the longest x1 20.2 us: per_device(): lax.all_to_all(send_area.reshape(groups, capacity, PIX), ('maprow', 'mapc...]
    all_to_all x3 -> x0, starting transfers between devices: 36.5 us -> none  [the longest x1 16.1 us: per_device(): lax.all_to_all(send_ids.reshape(groups, capacity), ('maprow', 'mapcol'),...]
    eq x17 -> x0, local copies, waits for them, and re-layouts: 14.4 us -> none  [the longest x16 13.6 us: pixel_table(): pixels[:, :, None] == jnp.arange(PIX, dtype=jnp.int32)[None, None, :]]
    reshape x6 -> x0, local copies, waits for them, and re-layouts: 12.7 us -> none  [the longest x2 6.51 us: blockify(): field.reshape(blocks_down, BR, blocks_across, BC).transpose(0, 2, 1, 3)]
    ppermute x4 -> x0, starting transfers between devices: 9.07 us -> none  [the longest x2 5.87 us: extended(): lax.ppermute(tail, axis, [(i, (i + 1) % count) for i in range(ends)])]
    transpose x3 -> x0, local copies, waits for them, and re-layouts: 8.66 us -> none  [the longest x2 5.91 us: blockify(): field.reshape(blocks_down, BR, blocks_across, BC).transpose(0, 2, 1, 3)]
  transfers between devices with their start and end apart: 7 -> 0, of which waited for: 2 -> 0; matrix products, arithmetic and copies ran while one was open for 34% -> 0% of each run, Pallas kernels for 0% -> 0%
where the time goes in v1:
time: 76 us; the launch traced here: 74.9 us
  Pallas kernels  68.3 us (90%)
  local copies, waits for them, and re-layouts  5.95 us (8%)
    pallas_call x1, Pallas kernels, per_device(): pl.pallas_call(functools.partial(exchange, nr, nz, cap), out_shape=(jax.S...  61.7 us
    pallas_call x1, Pallas kernels, per_device(): pl.pallas_call(functools.partial(lookup, rows // BR), out_shape=jax.Shape...  6.65 us
    unnamed x13, local copies, waits for them, and re-layouts  5.95 us

profile of v1, /device:TPU:32, one launch (start us, length us, event | category | flops | bytes accessed | tf_op | source)
XLA Modules:
  0.0 74.9 jit_solution(14774116372729856605)
XLA Ops:
  0.6 0.0 copy-start
  0.6 1.0 %copy-done = s32[256,512]{1,0:T(8,128)S(1)} copy-done((s32[256,512]{1,0:T(8,128)S(1)}, s32[256,512]{1,0:T(8,128)}, u32[]{:S(2)}) %copy-start) | copy-done | bytes 524312
  1.7 0.0 copy-start.1
  1.7 1.0 %copy-done.1 = f32[256,512]{1,0:T(8,128)S(1)} copy-done((f32[256,512]{1,0:T(8,128)S(1)}, f32[256,512]{1,0:T(8,128)}, u32[]{:S(2)}) %copy-start.1) | copy-done | bytes 524312
  2.7 0.0 copy-start.2
  2.7 1.0 %copy-done.2 = s32[256,512]{1,0:T(8,128)S(1)} copy-done((s32[256,512]{1,0:T(8,128)S(1)}, s32[256,512]{1,0:T(8,128)}, u32[]{:S(2)}) %copy-start.2) | copy-done | bytes 524312
  3.8 0.0 copy-start.3
  3.8 0.8 %copy-done.3 = f32[128,128]{1,0:T(8,128)S(1)} copy-done((f32[128,128]{1,0:T(8,128)S(1)}, f32[128,128]{1,0:T(8,128)}, u32[]{:S(2)}) %copy-start.3) | copy-done | bytes 65560
  4.6 0.0 copy-start.4
  4.6 0.7 copy-done.4
  5.3 0.0 copy-start.5
  5.3 0.7 copy-done.5
  6.0 61.7 %shard_map.77 = (f32[128,128]{1,0:T(8,128)S(1)}, f32[512,128]{1,0:T(8,128)S(1)}) custom-call(f32[256,512]{1,0:T(8,128)S(1)} %copy-done.1, s32[256,512]{1,0:T(8,128)S(1)} %copy-done.2, s32[256,512]{1,0:T(8,128)S(1)} %copy-done, s32[1,512]{1,0:T(1,128)S(1)} %bitcast.1, s32[1,512]{1,0:T(1,128)S(1)} %copy-done.5, f32[128,128]{1,0:T(8,128)S(1)} %copy-done.3), custom_call_target="tpu_custom_call" | custom-call | tf_op jit(solution)/shard_map/pallas_call | solution.py:373
  67.6 6.6 %shard_map.78 = f32[256,512]{1,0:T(8,128)} custom-call(f32[512,128]{1,0:T(8,128)S(1)} %get-tuple-element.5.found, s32[256,512]{1,0:T(8,128)S(1)} %copy-done), custom_call_target="tpu_custom_call" | custom-call | tf_op jit(solution)/shard_map/pallas_call | solution.py:421
  74.3 0.6 copy.9
Async XLA Ops:
  0.6 1.0 %copy-start = (s32[256,512]{1,0:T(8,128)S(1)}, s32[256,512]{1,0:T(8,128)}, u32[]{:S(2)}) copy-start(s32[256,512]{1,0:T(8,128)} %pix.3) | copy-start | bytes 1572868
  1.7 1.0 %copy-start.1 = (f32[256,512]{1,0:T(8,128)S(1)}, f32[256,512]{1,0:T(8,128)}, u32[]{:S(2)}) copy-start(f32[256,512]{1,0:T(8,128)} %elev.1) | copy-start | bytes 1572868
  2.7 1.0 %copy-start.2 = (s32[256,512]{1,0:T(8,128)S(1)}, s32[256,512]{1,0:T(8,128)}, u32[]{:S(2)}) copy-start(s32[256,512]{1,0:T(8,128)} %lay.1) | copy-start | bytes 1572868
  3.8 0.8 %copy-start.3 = (f32[128,128]{1,0:T(8,128)S(1)}, f32[128,128]{1,0:T(8,128)}, u32[]{:S(2)}) copy-start(f32[128,128]{1,0:T(8,128)} %back.1) | copy-start | bytes 196612
  4.6 0.7 copy-start.4
  5.3 0.7 copy-start.5

commit v2 on v1

--- a/solution.py
+++ b/solution.py
@@ -50,23 +50,29 @@
     return lax.dot_general(a, b, (((1,), (1,)), ((), ())), preferred_element_type=F32)
 
 
-def block_sums(area, pixel):
-    firsts, seconds, lows = [], [], []
+def pixel_side(pixel):
+    places = [swap_groups(pixel[8 * half : 8 * half + 8]) for half in range(2)]
+    lows = [
+        jnp.where((p & 15)[:, None, :] == iota((8, 16, 128), 1), 1.0, 0.0).reshape(128, 128)
+        for p in places
+    ]
+    return jnp.concatenate(places, axis=1), jnp.concatenate(lows, axis=1).astype(BF16)
+
+
+def block_sums(area, places, lows):
+    firsts, seconds = [], []
     for half in range(2):
         a = swap_groups(area[8 * half : 8 * half + 8])
-        p = swap_groups(pixel[8 * half : 8 * half + 8])
+        high = places[:, 128 * half : 128 * half + 128] >> 4
         a1 = a.astype(BF16).astype(F32)
         a2 = a - a1
-        is_high = (p >> 4)[:, None, :] == iota((8, 8, 128), 1)
-        is_low = (p & 15)[:, None, :] == iota((8, 16, 128), 1)
+        is_high = high[:, None, :] == iota((8, 8, 128), 1)
         firsts.append(jnp.where(is_high, a1[:, None, :], 0.0).reshape(64, 128))
         seconds.append(jnp.where(is_high, a2[:, None, :], 0.0).reshape(64, 128))
-        lows.append(jnp.where(is_low, 1.0, 0.0).reshape(128, 128))
     left = jnp.concatenate(
         [jnp.concatenate(firsts, axis=1), jnp.concatenate(seconds, axis=1)], axis=0
     ).astype(BF16)
-    right = jnp.concatenate(lows, axis=1).astype(BF16)
-    out = dot_nt(left, right)
+    out = dot_nt(left, lows)
     out = out[:64] + out[64:]
     group = iota((8, 128), 1) >> 4
     own = out[0:8]
@@ -77,15 +83,15 @@
 
 def exchange(
     nr, nz, cap,
-    elev, lay, pix, target, local, back,
-    gamma, found,
-    epad, layv, pixv, look, pmat, pmt, oht, oh, hist, sendb, recvb, idsend, idrecv,
+    elev, lay, pix, target_in, local_in, back_in,
+    gamma, found, places,
+    target, local, back, low_table, epad, layv, pixv, look, pmat, pmt, oht, oh, hist, sendb, recvb, idsend, idrecv,
     dense, cin, gin, backb, retb,
     in_sem, halo_send, halo_recv, id_send, id_recv, out_send, out_recv,
     chain_send, chain_recv, gchain_send, gchain_recv, ret_send, ret_recv,
 ):
     rows, cols = elev.shape
-    tb = target.shape[1]
+    tb = target_in.shape[1]
     dests = nr * nz
     h = nz // 2
     tiles = cols // 128
@@ -112,13 +118,18 @@
         pl.semaphore_signal(barrier, inc=1, device_id=neighbour, device_id_type=MESH)
 
     loads = [
-        pltpu.make_async_copy(elev, epad.at[8 : 8 + rows, 128 : 128 + cols], in_sem.at[0]),
-        pltpu.make_async_copy(lay, layv, in_sem.at[1]),
+        pltpu.make_async_copy(target_in, target, in_sem.at[0]),
+        pltpu.make_async_copy(local_in, local, in_sem.at[1]),
         pltpu.make_async_copy(pix, pixv, in_sem.at[2]),
+        pltpu.make_async_copy(elev, epad.at[8 : 8 + rows, 128 : 128 + cols], in_sem.at[3]),
+        pltpu.make_async_copy(lay, layv, in_sem.at[4]),
+        pltpu.make_async_copy(back_in, back, in_sem.at[5]),
     ]
     for load in loads:
         load.start()
 
+    loads[0].wait()
+    loads[1].wait()
     name = target[...]
     step_z = ((name & (nz - 1)) + (nz - c)) & (nz - 1)
     ahead = step_z - h
@@ -169,16 +180,25 @@
 
     to_plane(lambda i: idsend.at[i], lambda i: idrecv.at[i], id_send.at[0], id_recv.at[0])
 
+    loads[2].wait()
+    group_bands = 8 if rows % (8 * BR) == 0 else 2
+
+    def pixels(i, carry):
+        for n in range(group_bands):
+            top = pl.multiple_of(i * (group_bands * BR) + n * BR, BR)
+            for j in range(tiles):
+                unit = i * (group_bands * tiles) + n * tiles + j
+                place, low = pixel_side(pixv[pl.ds(top, BR), 128 * j : 128 * j + 128])
+                places[pl.ds(pl.multiple_of(8 * unit, 8), 8), :] = place
+                low_table[unit] = low
+        return carry
+
+    lax.fori_loop(0, rows // (group_bands * BR), pixels, 0)
+
     i0 = iota((128, 1), 0)
     row_slot = ((i0 // cap) * (nz * cap) + lax.rem(i0, cap)).astype(F32)
-    i1 = iota((1, 128), 1)
-    lane_slot = ((i1 // cap) * (nz * cap) + lax.rem(i1, cap)).astype(F32)
-    slot_down = jnp.transpose(jnp.broadcast_to(slot, (128, tb)))
     for p in range(nz):
         pmat[p] = jnp.where(row_slot + float(p * cap) == slot, 1.0, 0.0).astype(BF16)
-        pmt[:, 128 * p : 128 * p + 128] = jnp.where(
-            slot_down == lane_slot + float(p * cap), 1.0, 0.0
-        ).astype(BF16)
 
     column = ((c * 2 + s) * cols + iota((1, cols), 1)).astype(F32)
     incidence = 0.52 + 0.28 * (column + 0.5) / float(cols * nz * 2)
@@ -187,8 +207,8 @@
     look[1:2, :] = -sine * jnp.sin(heading) / (2.0 * CELL_SPACING)
     look[2:3, :] = jnp.cos(incidence)
 
-    for load in loads:
-        load.wait()
+    loads[3].wait()
+    loads[4].wait()
     for halo in halos:
         halo.wait_recv()
 
@@ -208,30 +228,32 @@
     def _():
         epad[8 : 8 + rows, 128 + cols : 256 + cols] = jnp.zeros((rows, 128), F32)
 
-    def band(i, carry):
-        top = pl.multiple_of(i * BR, BR)
+    def bands(i, carry):
         lane = iota((BR, 128), 1)
-        around = epad[pl.ds(top, 32), 128 : 128 + cols]
-        mid = epad[pl.ds(pl.multiple_of(top + 8, 8), BR), :]
-        mids = [mid[:, 128 * j : 128 * j + 128] for j in range(tiles + 2)]
-        right = [pltpu.roll(x, 1, 1) for x in mids[:-1]]
-        left = [pltpu.roll(x, 127, 1) for x in mids[1:]]
-        for j in range(tiles):
-            at = slice(128 * j, 128 * j + 128)
-            before = jnp.where(lane == 0, right[j], right[j + 1])
-            after = jnp.where(lane == 127, left[j + 1], left[j])
-            rise_cols = after - before
-            rise_rows = around[9:25, at] - around[7:23, at]
-            facing = (
-                look[2:3, at] - rise_cols * look[0:1, at] - rise_rows * look[1:2, at]
-            )
-            lit = (1 - layv[pl.ds(top, BR), at]).astype(F32)
-            area = jnp.maximum(facing, 0.0) * lit
-            sums = block_sums(area, pixv[pl.ds(top, BR), at])
-            hist[pl.ds(pl.multiple_of(i * (tiles * 8) + 8 * j, 8), 8), :] = sums
+        for n in range(group_bands):
+            top = pl.multiple_of(i * (group_bands * BR) + n * BR, BR)
+            around = epad[pl.ds(top, 32), 128 : 128 + cols]
+            mid = epad[pl.ds(pl.multiple_of(top + 8, 8), BR), :]
+            mids = [mid[:, 128 * j : 128 * j + 128] for j in range(tiles + 2)]
+            right = [pltpu.roll(x, 1, 1) for x in mids[:-1]]
+            left = [pltpu.roll(x, 127, 1) for x in mids[1:]]
+            for j in range(tiles):
+                at = slice(128 * j, 128 * j + 128)
+                unit = i * (group_bands * tiles) + n * tiles + j
+                span = pl.ds(pl.multiple_of(8 * unit, 8), 8)
+                before = jnp.where(lane == 0, right[j], right[j + 1])
+                after = jnp.where(lane == 127, left[j + 1], left[j])
+                rise_cols = after - before
+                rise_rows = around[9:25, at] - around[7:23, at]
+                facing = (
+                    look[2:3, at] - rise_cols * look[0:1, at] - rise_rows * look[1:2, at]
+                )
+                lit = (1 - layv[pl.ds(top, BR), at]).astype(F32)
+                area = jnp.maximum(facing, 0.0) * lit
+                hist[span, :] = block_sums(area, places[span, :], low_table[unit])
         return carry
 
-    lax.fori_loop(0, rows // BR, band, 0)
+    lax.fori_loop(0, rows // (group_bands * BR), bands, 0)
 
     terms = split(hist[...])
     for g, (p0, p1) in enumerate(spans):
@@ -243,6 +265,15 @@
             out_send.at[g], out_recv.at[g],
         )
 
+    i1 = iota((1, 128), 1)
+    lane_slot = ((i1 // cap) * (nz * cap) + lax.rem(i1, cap)).astype(F32)
+    slot_down = jnp.transpose(jnp.broadcast_to(slot, (128, tb)))
+    for p in range(nz):
+        pmt[:, 128 * p : 128 * p + 128] = jnp.where(
+            slot_down == lane_slot + float(p * cap), 1.0, 0.0
+        ).astype(BF16)
+
+    loads[5].wait()
     arrived(idrecv.at[0 : nr - 1], id_recv.at[0])
     names = idrecv[0]
     for i in range(1, nr):
@@ -345,20 +376,26 @@
         one.wait_send()
 
 
-def lookup(bands, found, pix, out):
-    tiles = out.shape[1] // 128
-
-    def band(i, carry):
-        for j in range(tiles):
-            at = slice(128 * j, 128 * j + 128)
-            table = found[pl.ds(pl.multiple_of(i * (tiles * 8) + 8 * j, 8), 8), :]
-            for half in range(2):
-                span = pl.ds(pl.multiple_of(i * BR + 8 * half, 8), 8)
-                place = swap_groups(pix[span, at])
-                out[span, at] = swap_groups(jnp.take_along_axis(table, place, axis=1))
-        return carry
-
-    lax.fori_loop(0, bands, band, 0)
+def lookup(found, places, gamma, gamma_out, out, cells, sems):
+    rows, cols = out.shape
+    tiles = cols // 128
+    chunk = 64 if rows % 64 == 0 else rows
+    copies = [pltpu.make_async_copy(gamma, gamma_out, sems.at[0])]
+    copies[0].start()
+    for k in range(rows // chunk):
+        for i in range(k * (chunk // BR), (k + 1) * (chunk // BR)):
+            for j in range(tiles):
+                span = slice(8 * (i * tiles + j), 8 * (i * tiles + j) + 8)
+                for half in range(2):
+                    place = places[span, 128 * half : 128 * half + 128]
+                    value = jnp.take_along_axis(found[span, :], place, axis=1)
+                    top = BR * i + 8 * half
+                    cells[top : top + 8, 128 * j : 128 * j + 128] = swap_groups(value)
+        part = slice(k * chunk, (k + 1) * chunk)
+        copies.append(pltpu.make_async_copy(cells.at[part], out.at[part], sems.at[k + 1]))
+        copies[-1].start()
+    for copy in copies:
+        copy.wait()
 
 
 def per_device(nr, nz, elevation, layover, footprint_pixel, footprint_device, local_block, backscatter):
@@ -368,17 +405,22 @@
     h = nz // 2
     held = backscatter.shape[0]
     vmem = pl.BlockSpec(memory_space=pltpu.VMEM)
-    hbm = pl.BlockSpec(memory_space=pl.ANY)
+    hbm = pl.BlockSpec(memory_space=pltpu.HBM)
     dma = pltpu.SemaphoreType.DMA
-    gamma, found = pl.pallas_call(
+    gamma, found, places = pl.pallas_call(
         functools.partial(exchange, nr, nz, cap),
         out_shape=(
             jax.ShapeDtypeStruct((held, PIX), F32),
             jax.ShapeDtypeStruct((tb, PIX), F32),
+            jax.ShapeDtypeStruct((tb, BR * BC), jnp.int32),
         ),
-        in_specs=[hbm, hbm, hbm, vmem, vmem, vmem],
-        out_specs=(vmem, vmem),
+        in_specs=[hbm] * 6,
+        out_specs=(vmem, vmem, vmem),
         scratch_shapes=[
+            pltpu.VMEM((1, tb), jnp.int32),
+            pltpu.VMEM((1, tb), jnp.int32),
+            pltpu.VMEM((held, PIX), F32),
+            pltpu.VMEM((tb // 8, 128, BR * BC), BF16),
             pltpu.VMEM((rows + 16, cols + 256), F32),
             pltpu.VMEM((rows, cols), jnp.int32),
             pltpu.VMEM((rows, cols), jnp.int32),
@@ -397,7 +439,7 @@
             pltpu.VMEM((2, h + 1, 2, 64, PIX), F32),
             pltpu.VMEM((nr, nz, cap, PIX), F32),
             pltpu.VMEM((nr, nz, cap, PIX), F32),
-            dma((3,)),
+            dma((6,)),
             dma((4,)),
             dma((4,)),
             dma((1,)),
@@ -415,17 +457,25 @@
             collective_id=0, has_side_effects=True, vmem_limit_bytes=40 * 2**20
         ),
     )(
-        elevation, layover, footprint_pixel,
-        footprint_device.reshape(1, tb), local_block, backscatter,
+        *(
+            pltpu.with_memory_space_constraint(x, pltpu.HBM)
+            for x in (
+                elevation, layover, footprint_pixel,
+                footprint_device.reshape(1, tb), local_block, backscatter,
+            )
+        )
     )
-    gamma_map = pl.pallas_call(
-        functools.partial(lookup, rows // BR),
-        out_shape=jax.ShapeDtypeStruct((rows, cols), F32),
-        in_specs=[vmem, vmem],
-        out_specs=vmem,
-        compiler_params=pltpu.CompilerParams(vmem_limit_bytes=16 * 2**20),
-    )(found, footprint_pixel)
-    return gamma, gamma_map
+    return pl.pallas_call(
+        lookup,
+        out_shape=(
+            jax.ShapeDtypeStruct((held, PIX), F32),
+            jax.ShapeDtypeStruct((rows, cols), F32),
+        ),
+        in_specs=[vmem, vmem, vmem],
+        out_specs=(hbm, hbm),
+        scratch_shapes=[pltpu.VMEM((rows, cols), F32), dma((1 + max(1, rows // 64),))],
+        compiler_params=pltpu.CompilerParams(vmem_limit_bytes=8 * 2**20),
+    )(found, places, gamma)
 
 
 def solution(mesh):

time: 76 us -> 63.7 us (0.84)
  Pallas kernels: 68.3 us -> 62.2 us
  local copies, waits for them, and re-layouts: 5.95 us -> 0 us
    unnamed x13 -> x0, local copies, waits for them, and re-layouts: 5.95 us -> none
    pallas_call x1, Pallas kernels: 61.7 us -> 55.7 us  [per_device(): pl.pallas_call(functools.partial(exchange, nr, nz, cap), out_shape=(jax.S...]
where the time goes in v2:
time: 63.7 us; the launch traced here: 62.8 us
  Pallas kernels  62.2 us (98%)
  between operations  0.64 us (1%)
    pallas_call x1, Pallas kernels, per_device(): pl.pallas_call(functools.partial(exchange, nr, nz, cap), out_shape=(jax.S...  55.7 us
    pallas_call x1, Pallas kernels, per_device(): pl.pallas_call(lookup, out_shape=(jax.ShapeDtypeStruct((held, PIX), F32),...  6.46 us

profile of v2, /device:TPU:32, one launch (start us, length us, event | category | flops | bytes accessed | tf_op | source)
XLA Modules:
  0.0 62.8 jit_solution(8596192317920821120)
XLA Ops:
  0.6 55.7 %shard_map.77 = (f32[128,128]{1,0:T(8,128)S(1)}, f32[512,128]{1,0:T(8,128)S(1)}, s32[512,256]{1,0:T(8,128)S(1)}) custom-call(f32[256,512]{1,0:T(8,128)} %elev.1, s32[256,512]{1,0:T(8,128)} %lay.1, s32[256,512]{1,0:T(8,128)} %pix.1, s32[1,512]{1,0:T(1,128)} %bitcast.1, s32[1,512]{1,0:T(1,128)} %local_in.1, f32[128,128]{1,0:T(8,128)} %back_in.1), custom_call_target="tpu_custom_call" | custom-call | tf_op jit(solution)/shard_map/pallas_call | solution.py:410
  56.4 6.5 %shard_map.78 = (f32[128,128]{1,0:T(8,128)}, f32[256,512]{1,0:T(8,128)}) custom-call(f32[512,128]{1,0:T(8,128)S(1)} %get-tuple-element.5.found, s32[512,256]{1,0:T(8,128)S(1)} %get-tuple-element.6.places, f32[128,128]{1,0:T(8,128)S(1)} %get-tuple-element.7.gamma), custom_call_target="tpu_custom_call" | custom-call | tf_op jit(solution)/shard_map/pallas_call | solution.py:468

commit v3 on v2

--- a/solution.py
+++ b/solution.py
@@ -81,41 +81,56 @@
     return swap_groups(own)
 
 
+STEP = (0, 2, -2, 1, 3, -1, -3, 4)
+SPANS = ((3, 5, 1), (5, 7, -1), (7, 8, 2), (0, 3, 0))
+TABLES = ((1, 4, 7), (2, 6, 7), (0, 3, 5))
+
+
 def exchange(
     nr, nz, cap,
     elev, lay, pix, target_in, local_in, back_in,
     gamma, found, places,
-    target, local, back, low_table, epad, layv, pixv, look, pmat, pmt, oht, oh, hist, sendb, recvb, idsend, idrecv,
-    dense, cin, gin, backb, retb,
+    target, local, back, low_table, epad, layv, pixv, look, put_low, put_high, pick, oht, oh, hist,
+    sendb, recvb, idsend, idrecv, partial, cin, packed, gin, backb, retb,
     in_sem, halo_send, halo_recv, id_send, id_recv, out_send, out_recv,
-    chain_send, chain_recv, gchain_send, gchain_recv, ret_send, ret_recv,
+    sum_send, sum_recv, gam_send, gam_recv, ret_send, ret_recv,
 ):
     rows, cols = elev.shape
     tb = target_in.shape[1]
     dests = nr * nz
-    h = nz // 2
+    hc = cap // 2
+    n4 = nr * hc
     tiles = cols // 128
     r, c, s = lax.axis_index("maprow"), lax.axis_index("mapcol"), lax.axis_index("sect")
-    up_z, down_z = {"mapcol": lax.rem(c + 1, nz)}, {"mapcol": lax.rem(c + nz - 1, nz)}
+
+    def plane(step):
+        return lax.rem(c + (step + nz), nz)
+
     west = {"mapcol": lax.rem(c + nz - 1 + s, nz), "sect": 1 - s}
     east = {"mapcol": lax.rem(c + s, nz), "sect": 1 - s}
     north, south = {"maprow": lax.rem(r + nr - 1, nr)}, {"maprow": lax.rem(r + 1, nr)}
-    spans = [(0, 1)] + [(2 * g - 1, 2 * g + 1) for g in range(1, h)] + [(nz - 1, nz)]
-
-    def place(k):
-        return 2 * (k - h) if k >= h else 2 * (h - k) - 1
 
     barrier = pltpu.get_barrier_semaphore()
 
     def greet(j, carry):
+        peer = lax.rem(r + j, nr)
+        for step in (1, -1, 2, -2):
+            pl.semaphore_signal(
+                barrier, inc=1, device_id={"maprow": peer, "mapcol": plane(step)},
+                device_id_type=MESH,
+            )
+        return carry
+
+    def greet_plane(j, carry):
         pl.semaphore_signal(
             barrier, inc=1, device_id={"maprow": lax.rem(r + j, nr)}, device_id_type=MESH
         )
         return carry
 
-    lax.fori_loop(1, nr, greet, 0)
-    for neighbour in (up_z, down_z, west, east):
+    for neighbour in (west, east):
         pl.semaphore_signal(barrier, inc=1, device_id=neighbour, device_id_type=MESH)
+    lax.fori_loop(1, nr, greet_plane, 0)
+    lax.fori_loop(0, nr, greet, 0)
 
     loads = [
         pltpu.make_async_copy(target_in, target, in_sem.at[0]),
@@ -131,9 +146,10 @@
     loads[0].wait()
     loads[1].wait()
     name = target[...]
-    step_z = ((name & (nz - 1)) + (nz - c)) & (nz - 1)
-    ahead = step_z - h
-    order = jnp.where(ahead >= 0, 2 * ahead, -2 * ahead - 1)
+    ahead = ((name & (nz - 1)) + (nz - c)) & (nz - 1)
+    order = jnp.zeros((1, tb), jnp.int32)
+    for p, step in enumerate(STEP):
+        order = jnp.where(ahead == step % nz, p, order)
     spot = (name >> (nz.bit_length() - 1)) * nz + order
     onehot = iota((dests, tb), 0) == spot
     earlier = jnp.where(iota((tb, tb), 0) < iota((tb, tb), 1), 1.0, 0.0).astype(BF16)
@@ -141,12 +157,14 @@
     rank = jnp.sum(jnp.where(onehot, running, 0.0), axis=0, keepdims=True)
     slot = (spot * cap).astype(F32) + rank
     ids = jnp.where(onehot, local[...].astype(F32), 0.0).astype(BF16)
-    at_lane = (r * cap).astype(F32) + rank
+    high = rank >= float(hc)
+    within = jnp.where(high, rank - float(hc), rank)
+    at_lane = (r * hc).astype(F32) + within + jnp.where(high, float(n4), 0.0)
     lanes = jnp.where(iotaf((128, tb), 0) == at_lane, 1.0, 0.0).astype(BF16)
     idsend[...] = dot_nt(ids, lanes).reshape(nr, nz, 128)
-    idrecv[pl.ds(r, 1)] = idsend[pl.ds(r, 1)]
-
-    pl.semaphore_wait(barrier, nr - 1 + 4)
+    idrecv[pl.ds(r, 1), 0:3] = idsend[pl.ds(r, 1), 0:3]
+
+    pl.semaphore_wait(barrier, 5 * nr - 1 + 2)
 
     halos = [
         (elev.at[rows - 8 : rows, :], epad.at[0:8, 128 : 128 + cols], south),
@@ -164,21 +182,45 @@
     for halo in halos:
         halo.start()
 
-    def to_plane(source, sink, send_sem, recv_sem):
-        def body(j, carry):
-            peer = lax.rem(r + j, nr)
+    def to_peers(source, sink, send_sem, recv_sem, way):
+        def start(span, peer):
+            p0, p1, step = span
+            where = plane(way * step)
+            if step == 2:
+                where = jnp.where((r + peer) % 2 == 0, plane(2 * way), plane(-2 * way))
+            k = 0 if step == 0 else 1
             pltpu.make_async_remote_copy(
-                src_ref=source(peer), dst_ref=sink(r), send_sem=send_sem, recv_sem=recv_sem,
-                device_id={"maprow": peer}, device_id_type=MESH,
+                src_ref=source(p0, p1, peer), dst_ref=sink(p0, p1, r),
+                send_sem=send_sem.at[k], recv_sem=recv_sem.at[k],
+                device_id={"maprow": peer, "mapcol": where}, device_id_type=MESH,
             ).start()
+
+        def far(j, carry):
+            for span in SPANS[:3]:
+                start(span, lax.rem(r + j, nr))
             return carry
 
-        lax.fori_loop(1, nr, body, 0)
-
-    def arrived(part, sem):
+        def near(j, carry):
+            start(SPANS[3], lax.rem(r + j, nr))
+            return carry
+
+        lax.fori_loop(0, nr, far, 0)
+        lax.fori_loop(1, nr, near, 0)
+
+    def done(part, sem):
         pltpu.make_async_copy(part, part, sem).wait()
 
-    to_plane(lambda i: idsend.at[i], lambda i: idrecv.at[i], id_send.at[0], id_recv.at[0])
+    def done_rows(buffer, sem):
+        done(buffer.at[3:nz], sem.at[1])
+        done(buffer.at[0:3, 0 : (nr - 1) * hc], sem.at[0])
+
+    def of_rows(buffer):
+        return lambda p0, p1, i: buffer.at[p0:p1, pl.ds(i * hc, hc)]
+
+    to_peers(
+        lambda p0, p1, i: idsend.at[i, p0:p1], lambda p0, p1, i: idrecv.at[i, p0:p1],
+        id_send, id_recv, 1,
+    )
 
     loads[2].wait()
     group_bands = 8 if rows % (8 * BR) == 0 else 2
@@ -195,10 +237,10 @@
 
     lax.fori_loop(0, rows // (group_bands * BR), pixels, 0)
 
-    i0 = iota((128, 1), 0)
-    row_slot = ((i0 // cap) * (nz * cap) + lax.rem(i0, cap)).astype(F32)
-    for p in range(nz):
-        pmat[p] = jnp.where(row_slot + float(p * cap) == slot, 1.0, 0.0).astype(BF16)
+    i0 = iota((nz * n4, 1), 0)
+    row_slot = (((i0 % n4) // hc) * (nz * cap) + (i0 // n4) * cap + i0 % hc).astype(F32)
+    put_low[...] = jnp.where(row_slot == slot, 1.0, 0.0).astype(BF16)
+    put_high[...] = jnp.where(row_slot + float(hc) == slot, 1.0, 0.0).astype(BF16)
 
     column = ((c * 2 + s) * cols + iota((1, cols), 1)).astype(F32)
     incidence = 0.52 + 0.28 * (column + 0.5) / float(cols * nz * 2)
@@ -255,124 +297,149 @@
 
     lax.fori_loop(0, rows // (group_bands * BR), bands, 0)
 
-    terms = split(hist[...])
-    for g, (p0, p1) in enumerate(spans):
-        for p in range(p0, p1):
-            sendb[:, p] = folded(dot(pmat[p], terms)).reshape(nr, cap, PIX)
-        recvb[pl.ds(r, 1), p0:p1] = sendb[pl.ds(r, 1), p0:p1]
-        to_plane(
-            lambda i: sendb.at[i, p0:p1], lambda i: recvb.at[i, p0:p1],
-            out_send.at[g], out_recv.at[g],
-        )
-
-    i1 = iota((1, 128), 1)
-    lane_slot = ((i1 // cap) * (nz * cap) + lax.rem(i1, cap)).astype(F32)
-    slot_down = jnp.transpose(jnp.broadcast_to(slot, (128, tb)))
-    for p in range(nz):
-        pmt[:, 128 * p : 128 * p + 128] = jnp.where(
-            slot_down == lane_slot + float(p * cap), 1.0, 0.0
+    left = iota((nz * n4, 128), 1) < 64
+    sums = hist[...]
+    lower = folded(dot(put_low[...], split(sums)))
+    upper = folded(dot(put_high[...], split(pltpu.roll(sums, 64, 1))))
+    sendb[0] = jnp.where(left, lower, upper).reshape(nz, n4, 128)
+    sendb[1] = jnp.where(left, upper, lower).reshape(nz, n4, 128)
+    mine = pl.ds(r * hc, hc)
+    for q in range(2):
+        recvb[q, 0:3, mine] = sendb[q, 0:3, mine]
+        to_peers(of_rows(sendb.at[q]), of_rows(recvb.at[q]), out_send.at[q], out_recv.at[q], 1)
+
+    row_of = (
+        within
+        + (((spot & (nz - 1)) * nr + (spot >> (nz.bit_length() - 1))) * hc).astype(F32)
+        + jnp.where(high, float(nz * n4), 0.0)
+    )
+    row_down = jnp.transpose(jnp.broadcast_to(row_of, (128, tb)))
+    high_down = row_down >= float(nz * n4)
+    row_down = jnp.where(high_down, row_down - float(nz * n4), row_down)
+    for n in range(0, nz * n4, 128):
+        width = min(128, nz * n4 - n)
+        pick[:, n : n + width] = jnp.where(
+            row_down[:, :width] == iotaf((1, width), 1) + float(n), 1.0, 0.0
         ).astype(BF16)
 
     loads[5].wait()
-    arrived(idrecv.at[0 : nr - 1], id_recv.at[0])
+    done(idrecv.at[:, 3:nz], id_recv.at[1])
+    done(idrecv.at[0 : nr - 1, 0:3], id_recv.at[0])
     names = idrecv[0]
     for i in range(1, nr):
         names = names + idrecv[i]
-    for p in range(nz):
-        wide = jnp.broadcast_to(names[p : p + 1, :], (128, 128))
-        oht[p] = jnp.where(wide == iotaf((128, 128), 0), 1.0, 0.0).astype(BF16)
-        oh[p] = jnp.where(jnp.transpose(wide) == iotaf((128, 128), 1), 1.0, 0.0).astype(BF16)
-
-    def hop(source, sinks, sends, recvs, way, j, q):
+    lane = iota((1, 128), 1)
+    even = ((lane % n4) // hc + r) % 2 == 0
+    for t, table in enumerate(TABLES):
+        for m, p in enumerate(table):
+            name = names[p : p + 1, :]
+            if p == 7:
+                name = jnp.where(even == (t == 0), name, -1.0)
+            if 2 * n4 < 128:
+                name = jnp.where(lane < 2 * n4, name, -1.0)
+            wide = jnp.broadcast_to(name, (128, 128))
+            at = slice(128 * m, 128 * m + 128)
+            oht[t, :, at] = jnp.where(wide == iotaf((128, 128), 0), 1.0, 0.0).astype(BF16)
+            oh[t, at, :] = jnp.where(
+                jnp.transpose(wide) == iotaf((128, 128), 1), 1.0, 0.0
+            ).astype(BF16)
+    half = iota((64, 128), 1) < 64
+    backs = [back[0:64, :], back[64:128, :]]
+    backs = [
+        jnp.where(half, backs[0], pltpu.roll(backs[1], 64, 1)),
+        jnp.where(half, pltpu.roll(backs[0], 64, 1), backs[1]),
+    ]
+
+    def filled(x):
+        if 2 * n4 == 128:
+            return x
+        return jnp.concatenate([x, jnp.zeros((128 - 2 * n4, 128), F32)], axis=0)
+
+    def table_of(q, t):
+        given = []
+        for p in TABLES[t]:
+            x = recvb[q, p]
+            y = pltpu.roll(x, 64, 1)
+            given.append(split(filled(jnp.concatenate([x, y] if q == 0 else [y, x], axis=0))))
+        total = folded(dot(oht[t], jnp.concatenate(given, axis=0)))
+        return jnp.where(half, total[0:64], pltpu.roll(total[64:128], 64, 1))
+
+    def two_steps(source, sink, send_sem, recv_sem, way):
         return pltpu.make_async_remote_copy(
-            src_ref=source, dst_ref=sinks.at[way, j, q],
-            send_sem=sends.at[way, j, q], recv_sem=recvs.at[way, j, q],
-            device_id=(up_z, down_z)[way], device_id_type=MESH,
+            src_ref=source, dst_ref=sink.at[way],
+            send_sem=send_sem.at[way], recv_sem=recv_sem.at[way],
+            device_id={"mapcol": plane((2, -2)[way])}, device_id_type=MESH,
         )
 
-    def pieces(j, last):
-        if j == last:
-            return [(0, 0), (1, 1)]
-        return [(w, q) for q in range(2) for w in range(2)]
-
-    hops = {}
-    for g, (p0, p1) in enumerate(spans):
-        arrived(recvb.at[0 : nr - 1, p0:p1], out_recv.at[g])
-        for p in range(p0, p1):
-            dense[p] = folded(dot(oht[p], split(recvb[:, p].reshape(128, PIX))))
-        if g < h:
-            for way, q in pieces(g + 1, 1):
-                p = place(h - g if way == 0 else h + g)
-                part = slice(64 * q, 64 * q + 64)
-                if (way, g, q) in hops:
-                    hops[way, g, q].wait_recv()
-                    dense[p, part] = dense[p, part] + cin[way, g, q]
-                hops[way, g + 1, q] = hop(
-                    dense.at[p, part], cin, chain_send, chain_recv, way, g + 1, q
-                )
-                hops[way, g + 1, q].start()
+    hops = []
+    own = []
+    for q in range(2):
+        done_rows(recvb.at[q], out_recv.at[q])
+        for way in range(2):
+            partial[q, way] = table_of(q, way)
+            hops.append(
+                two_steps(partial.at[q, way], cin.at[q], sum_send.at[q], sum_recv.at[q], way)
+            )
+            hops[-1].start()
+        own.append(table_of(q, 2))
+    gammas = []
+    for q in range(2):
+        hops[2 * q].wait_recv()
+        hops[2 * q + 1].wait_recv()
+        total = own[q] + cin[q, 0] + cin[q, 1]
+        packed[q] = backs[q] / jnp.maximum(total, 1.0)
+        for way in range(2):
+            gammas.append(
+                two_steps(packed.at[q], gin.at[q], gam_send.at[q], gam_recv.at[q], way)
+            )
+            gammas[-1].start()
+    halves = [(packed[q], pltpu.roll(packed[q], 64, 1)) for q in range(2)]
+    gamma[0:64] = jnp.where(half, halves[0][0], halves[1][1])
+    gamma[64:128] = jnp.where(half, halves[0][1], halves[1][0])
+
+    def served(q, t):
+        x = packed[q] if t == 2 else gin[q, 1 - t]
+        y = pltpu.roll(x, 64, 1)
+        whole = jnp.concatenate([jnp.where(half, x, y), jnp.where(half, y, x)], axis=0)
+        asked = folded(dot(oh[t], split(whole)))
+        slots = iota((n4, 128), 1) < 64
+        return [
+            jnp.where(
+                slots, asked[128 * m : 128 * m + n4], asked[128 * m + n4 : 128 * m + 2 * n4]
+            )
+            for m in range(3)
+        ]
+
+    for q in range(2):
+        for p, x in zip(TABLES[2], served(q, 2)):
+            backb[q, p] = x
+        gammas[2 * q].wait_recv()
+        gammas[2 * q + 1].wait_recv()
+        ahead_rows, behind_rows = served(q, 0), served(q, 1)
+        backb[q, 1], backb[q, 4] = ahead_rows[0], ahead_rows[1]
+        backb[q, 2], backb[q, 6] = behind_rows[0], behind_rows[1]
+        backb[q, 7] = ahead_rows[2] + behind_rows[2]
+        retb[q, 0:3, mine] = backb[q, 0:3, mine]
+        to_peers(of_rows(backb.at[q]), of_rows(retb.at[q]), ret_send.at[q], ret_recv.at[q], -1)
+
+    left = iota((tb, 128), 1) < 64
+    for q in range(2):
+        done_rows(retb.at[q], ret_recv.at[q])
+        x = folded(dot(pick[...], split(retb[q].reshape(nz * n4, 128))))
+        y = pltpu.roll(x, 64, 1)
+        if q == 0:
+            found[...] = jnp.where(high_down, y, x)
         else:
-            for q in range(2):
-                part = slice(64 * q, 64 * q + 64)
-                total = dense[p0, part]
-                for way in range(2):
-                    if (way, g, q) in hops:
-                        hops[way, g, q].wait_recv()
-                        total = total + cin[way, g, q]
-                gamma[part] = back[part] / jnp.maximum(total, 1.0)
-
-    ghops = {}
-
-    def pass_on(j):
-        for way, q in pieces(j, h):
-            source = gamma.at[64 * q : 64 * q + 64] if j == 1 else gin.at[way, j - 1, q]
-            if j > 1:
-                ghops[way, j - 1, q].wait_recv()
-            ghops[way, j, q] = hop(source, gin, gchain_send, gchain_recv, way, j, q)
-            ghops[way, j, q].start()
-
-    def give(g, tables):
-        p0, p1 = spans[g]
-        for p, table in zip(range(p0, p1), tables):
-            backb[:, p] = folded(dot(oh[p], split(table))).reshape(nr, cap, PIX)
-        retb[pl.ds(r, 1), p0:p1] = backb[pl.ds(r, 1), p0:p1]
-        to_plane(
-            lambda i: backb.at[i, p0:p1], lambda i: retb.at[i, p0:p1],
-            ret_send.at[g], ret_recv.at[g],
-        )
-
-    def take(g):
-        p0, p1 = spans[g]
-        arrived(retb.at[0 : nr - 1, p0:p1], ret_recv.at[g])
-        given = jnp.concatenate(
-            [split(retb[:, p].reshape(128, PIX)) for p in range(p0, p1)], axis=0
-        )
-        rows_found = folded(dot(pmt[:, 128 * p0 : 128 * p1], given))
-        found[...] = rows_found if g == h else found[...] + rows_found
-
-    pass_on(1)
-    give(h, [gamma[...]])
-    for j in range(1, h):
-        pass_on(j + 1)
-        for way, q in pieces(j, h):
-            if (way, j + 1, q) not in ghops:
-                ghops[way, j, q].wait_recv()
-        give(h - j, [gin[1, j].reshape(128, PIX), gin[0, j].reshape(128, PIX)])
-        take(h - j + 1)
-    for way, q in pieces(h, h):
-        ghops[way, h, q].wait_recv()
-    give(0, [jnp.concatenate([gin[0, h, 0], gin[1, h, 1]], axis=0)])
-    if h > 1:
-        take(1)
-    take(0)
+            found[...] = jnp.where(left, found[...], jnp.where(high_down, x, y))
 
     for halo in halos:
         halo.wait_send()
-    arrived(idsend.at[0 : nr - 1], id_send.at[0])
-    for g, (p0, p1) in enumerate(spans):
-        arrived(sendb.at[0 : nr - 1, p0:p1], out_send.at[g])
-        arrived(backb.at[0 : nr - 1, p0:p1], ret_send.at[g])
-    for one in (*hops.values(), *ghops.values()):
+    done(idsend.at[:, 3:nz], id_send.at[1])
+    done(idsend.at[0 : nr - 1, 0:3], id_send.at[0])
+    for q in range(2):
+        done_rows(sendb.at[q], out_send.at[q])
+        done_rows(backb.at[q], ret_send.at[q])
+    for one in (*hops, *gammas):
         one.wait_send()
 
 
@@ -382,15 +449,19 @@
     chunk = 64 if rows % 64 == 0 else rows
     copies = [pltpu.make_async_copy(gamma, gamma_out, sems.at[0])]
     copies[0].start()
+    for unit in range(rows // BR * tiles):
+        span = slice(8 * unit, 8 * unit + 8)
+        for half in range(2):
+            place = places[span, 128 * half : 128 * half + 128]
+            top, at = BR * (unit // tiles) + 8 * half, 128 * (unit % tiles)
+            cells[top : top + 8, at : at + 128] = jnp.take_along_axis(
+                found[span, :], place, axis=1
+            )
     for k in range(rows // chunk):
-        for i in range(k * (chunk // BR), (k + 1) * (chunk // BR)):
-            for j in range(tiles):
-                span = slice(8 * (i * tiles + j), 8 * (i * tiles + j) + 8)
-                for half in range(2):
-                    place = places[span, 128 * half : 128 * half + 128]
-                    value = jnp.take_along_axis(found[span, :], place, axis=1)
-                    top = BR * i + 8 * half
-                    cells[top : top + 8, 128 * j : 128 * j + 128] = swap_groups(value)
+        for top in range(k * chunk, (k + 1) * chunk, 8):
+            for at in range(0, cols, 128):
+                piece = (slice(top, top + 8), slice(at, at + 128))
+                cells[piece] = swap_groups(cells[piece])
         part = slice(k * chunk, (k + 1) * chunk)
         copies.append(pltpu.make_async_copy(cells.at[part], out.at[part], sems.at[k + 1]))
         copies[-1].start()
@@ -402,7 +473,7 @@
     rows, cols = elevation.shape
     tb = local_block.shape[1]
     cap = max(2, 2 * tb // (nr * nz))
-    h = nz // 2
+    n4 = nr * cap // 2
     held = backscatter.shape[0]
     vmem = pl.BlockSpec(memory_space=pltpu.VMEM)
     hbm = pl.BlockSpec(memory_space=pltpu.HBM)
@@ -425,33 +496,28 @@
             pltpu.VMEM((rows, cols), jnp.int32),
             pltpu.VMEM((rows, cols), jnp.int32),
             pltpu.VMEM((8, cols), F32),
-            pltpu.VMEM((nz, 128, tb), BF16),
-            pltpu.VMEM((tb, nz * 128), BF16),
-            pltpu.VMEM((nz, 128, 128), BF16),
-            pltpu.VMEM((nz, 128, 128), BF16),
+            pltpu.VMEM((nz * n4, tb), BF16),
+            pltpu.VMEM((nz * n4, tb), BF16),
+            pltpu.VMEM((tb, nz * n4), BF16),
+            pltpu.VMEM((3, 128, 3 * 128), BF16),
+            pltpu.VMEM((3, 3 * 128, 128), BF16),
             pltpu.VMEM((tb, PIX), F32),
-            pltpu.VMEM((nr, nz, cap, PIX), F32),
-            pltpu.VMEM((nr, nz, cap, PIX), F32),
+            pltpu.VMEM((2, nz, n4, 128), F32),
+            pltpu.VMEM((2, nz, n4, 128), F32),
             pltpu.VMEM((nr, nz, 128), F32),
             pltpu.VMEM((nr, nz, 128), F32),
-            pltpu.VMEM((nz, 128, PIX), F32),
-            pltpu.VMEM((2, h + 1, 2, 64, PIX), F32),
-            pltpu.VMEM((2, h + 1, 2, 64, PIX), F32),
-            pltpu.VMEM((nr, nz, cap, PIX), F32),
-            pltpu.VMEM((nr, nz, cap, PIX), F32),
+            pltpu.VMEM((2, 2, 64, 128), F32),
+            pltpu.VMEM((2, 2, 64, 128), F32),
+            pltpu.VMEM((2, 64, 128), F32),
+            pltpu.VMEM((2, 2, 64, 128), F32),
+            pltpu.VMEM((2, nz, n4, 128), F32),
+            pltpu.VMEM((2, nz, n4, 128), F32),
             dma((6,)),
             dma((4,)),
             dma((4,)),
-            dma((1,)),
-            dma((1,)),
-            dma((h + 1,)),
-            dma((h + 1,)),
-            dma((2, h + 1, 2)),
-            dma((2, h + 1, 2)),
-            dma((2, h + 1, 2)),
-            dma((2, h + 1, 2)),
-            dma((h + 1,)),
-            dma((h + 1,)),
+            dma((2,)),
+            dma((2,)),
+            *([dma((2, 2))] * 8),
         ],
         compiler_params=pltpu.CompilerParams(
             collective_id=0, has_side_effects=True, vmem_limit_bytes=40 * 2**20

time: 63.7 us -> 49.3 us (0.77)
  Pallas kernels: 62.2 us -> 48.2 us
    pallas_call x1, Pallas kernels: 55.7 us -> 46.7 us  [per_device(): pl.pallas_call(functools.partial(exchange, nr, nz, cap), out_shape=(jax.S...]
    pallas_call x1, Pallas kernels: 6.46 us -> 1.45 us  [per_device(): pl.pallas_call(lookup, out_shape=(jax.ShapeDtypeStruct((held, PIX), F32),...]
where the time goes in v3:
time: 49.3 us; the launch traced here: 48.8 us
  Pallas kernels  48.2 us (98%)
  between operations  0.64 us (1%)
    pallas_call x1, Pallas kernels, per_device(): pl.pallas_call(functools.partial(exchange, nr, nz, cap), out_shape=(jax.S...  46.7 us
    pallas_call x1, Pallas kernels, per_device(): pl.pallas_call(lookup, out_shape=(jax.ShapeDtypeStruct((held, PIX), F32),...  1.45 us

profile of v3, /device:TPU:32, one launch (start us, length us, event | category | flops | bytes accessed | tf_op | source)
XLA Modules:
  0.0 48.8 jit_solution(17525964511859046905)
XLA Ops:
  0.6 46.7 %shard_map.77 = (f32[128,128]{1,0:T(8,128)S(1)}, f32[512,128]{1,0:T(8,128)S(1)}, s32[512,256]{1,0:T(8,128)S(1)}) custom-call(f32[256,512]{1,0:T(8,128)} %elev.1, s32[256,512]{1,0:T(8,128)} %lay.1, s32[256,512]{1,0:T(8,128)} %pix.1, s32[1,512]{1,0:T(1,128)} %bitcast.1, s32[1,512]{1,0:T(1,128)} %local_in.1, f32[128,128]{1,0:T(8,128)} %back_in.1), custom_call_target="tpu_custom_call" | custom-call | tf_op jit(solution)/shard_map/pallas_call | solution.py:481
  47.4 1.4 %shard_map.78 = (f32[128,128]{1,0:T(8,128)}, f32[256,512]{1,0:T(8,128)}) custom-call(f32[512,128]{1,0:T(8,128)S(1)} %get-tuple-element.5.found, s32[512,256]{1,0:T(8,128)S(1)} %get-tuple-element.6.places, f32[128,128]{1,0:T(8,128)S(1)} %get-tuple-element.7.gamma), custom_call_target="tpu_custom_call" | custom-call | tf_op jit(solution)/shard_map/pallas_call | solution.py:534

commit v4 on v3

--- a/solution.py
+++ b/solution.py
@@ -91,8 +91,8 @@
     elev, lay, pix, target_in, local_in, back_in,
     gamma, found, places,
     target, local, back, low_table, epad, layv, pixv, look, put_low, put_high, pick, oht, oh, hist,
-    sendb, recvb, idsend, idrecv, partial, cin, packed, gin, backb, retb,
-    in_sem, halo_send, halo_recv, id_send, id_recv, out_send, out_recv,
+    edge_out, edge_in, sendb, recvb, idsend, idrecv, named, partial, cin, packed, gin, backb, retb,
+    in_sem, halo_send, halo_recv, id_send, id_recv, name_send, name_recv, out_send, out_recv,
     sum_send, sum_recv, gam_send, gam_recv, ret_send, ret_recv,
 ):
     rows, cols = elev.shape
@@ -106,6 +106,15 @@
     def plane(step):
         return lax.rem(c + (step + nz), nz)
 
+    def peer_of(i):
+        if nr != 16:
+            return lax.rem(r + 1 + i, nr)
+
+        def away(n):
+            return jnp.where(n == 0, 2, jnp.where(n == 3, 0, 2 * n - 1))
+
+        return (r // 4 + away(i // 4)) % 4 * 4 + (r % 4 + away(i % 4)) % 4
+
     west = {"mapcol": lax.rem(c + nz - 1 + s, nz), "sect": 1 - s}
     east = {"mapcol": lax.rem(c + s, nz), "sect": 1 - s}
     north, south = {"maprow": lax.rem(r + nr - 1, nr)}, {"maprow": lax.rem(r + 1, nr)}
@@ -113,8 +122,8 @@
     barrier = pltpu.get_barrier_semaphore()
 
     def greet(j, carry):
-        peer = lax.rem(r + j, nr)
-        for step in (1, -1, 2, -2):
+        peer = peer_of(j)
+        for step in (2, -2, 1, -1):
             pl.semaphore_signal(
                 barrier, inc=1, device_id={"maprow": peer, "mapcol": plane(step)},
                 device_id_type=MESH,
@@ -123,14 +132,14 @@
 
     def greet_plane(j, carry):
         pl.semaphore_signal(
-            barrier, inc=1, device_id={"maprow": lax.rem(r + j, nr)}, device_id_type=MESH
+            barrier, inc=1, device_id={"maprow": peer_of(j)}, device_id_type=MESH
         )
         return carry
 
     for neighbour in (west, east):
         pl.semaphore_signal(barrier, inc=1, device_id=neighbour, device_id_type=MESH)
-    lax.fori_loop(1, nr, greet_plane, 0)
     lax.fori_loop(0, nr, greet, 0)
+    lax.fori_loop(0, nr - 1, greet_plane, 0)
 
     loads = [
         pltpu.make_async_copy(target_in, target, in_sem.at[0]),
@@ -162,15 +171,35 @@
     at_lane = (r * hc).astype(F32) + within + jnp.where(high, float(n4), 0.0)
     lanes = jnp.where(iotaf((128, tb), 0) == at_lane, 1.0, 0.0).astype(BF16)
     idsend[...] = dot_nt(ids, lanes).reshape(nr, nz, 128)
-    idrecv[pl.ds(r, 1), 0:3] = idsend[pl.ds(r, 1), 0:3]
+    idrecv[pl.ds(r, 1)] = idsend[pl.ds(r, 1)]
+
+    loads[2].wait()
+    group_bands = 8 if rows % (8 * BR) == 0 else 2
+
+    def pixels(i, carry):
+        for n in range(group_bands):
+            top = pl.multiple_of(i * (group_bands * BR) + n * BR, BR)
+            for j in range(tiles):
+                unit = i * (group_bands * tiles) + n * tiles + j
+                place, low = pixel_side(pixv[pl.ds(top, BR), 128 * j : 128 * j + 128])
+                places[pl.ds(pl.multiple_of(8 * unit, 8), 8), :] = place
+                low_table[unit] = low
+        return carry
+
+    lax.fori_loop(0, rows // (group_bands * BR), pixels, 0)
+
+    loads[3].wait()
+    edge_out[0] = jnp.transpose(epad[8 : 8 + rows, 128:256])[0:8]
+    edge_out[1] = jnp.transpose(epad[8 : 8 + rows, cols : 128 + cols])[120:128]
 
     pl.semaphore_wait(barrier, 5 * nr - 1 + 2)
 
+    inner = slice(128, 128 + cols)
     halos = [
-        (elev.at[rows - 8 : rows, :], epad.at[0:8, 128 : 128 + cols], south),
-        (elev.at[0:8, :], epad.at[rows + 8 : rows + 16, 128 : 128 + cols], north),
-        (elev.at[:, cols - 128 : cols], epad.at[8 : 8 + rows, 0:128], east),
-        (elev.at[:, 0:128], epad.at[8 : 8 + rows, 128 + cols : 256 + cols], west),
+        (epad.at[rows : rows + 8, inner], epad.at[0:8, inner], south),
+        (epad.at[8:16, inner], epad.at[rows + 8 : rows + 16, inner], north),
+        (edge_out.at[0], edge_in.at[0], west),
+        (edge_out.at[1], edge_in.at[1], east),
     ]
     halos = [
         pltpu.make_async_remote_copy(
@@ -181,6 +210,16 @@
     ]
     for halo in halos:
         halo.start()
+
+    def name_slots(i, carry):
+        peer = peer_of(i)
+        pltpu.make_async_remote_copy(
+            src_ref=idsend.at[peer], dst_ref=idrecv.at[r], send_sem=id_send, recv_sem=id_recv,
+            device_id={"maprow": peer}, device_id_type=MESH,
+        ).start()
+        return carry
+
+    lax.fori_loop(0, nr - 1, name_slots, 0)
 
     def to_peers(source, sink, send_sem, recv_sem, way):
         def start(span, peer):
@@ -197,15 +236,15 @@
 
         def far(j, carry):
             for span in SPANS[:3]:
-                start(span, lax.rem(r + j, nr))
+                start(span, peer_of(j))
             return carry
 
         def near(j, carry):
-            start(SPANS[3], lax.rem(r + j, nr))
+            start(SPANS[3], peer_of(j))
             return carry
 
         lax.fori_loop(0, nr, far, 0)
-        lax.fori_loop(1, nr, near, 0)
+        lax.fori_loop(0, nr - 1, near, 0)
 
     def done(part, sem):
         pltpu.make_async_copy(part, part, sem).wait()
@@ -216,26 +255,6 @@
 
     def of_rows(buffer):
         return lambda p0, p1, i: buffer.at[p0:p1, pl.ds(i * hc, hc)]
-
-    to_peers(
-        lambda p0, p1, i: idsend.at[i, p0:p1], lambda p0, p1, i: idrecv.at[i, p0:p1],
-        id_send, id_recv, 1,
-    )
-
-    loads[2].wait()
-    group_bands = 8 if rows % (8 * BR) == 0 else 2
-
-    def pixels(i, carry):
-        for n in range(group_bands):
-            top = pl.multiple_of(i * (group_bands * BR) + n * BR, BR)
-            for j in range(tiles):
-                unit = i * (group_bands * tiles) + n * tiles + j
-                place, low = pixel_side(pixv[pl.ds(top, BR), 128 * j : 128 * j + 128])
-                places[pl.ds(pl.multiple_of(8 * unit, 8), 8), :] = place
-                low_table[unit] = low
-        return carry
-
-    lax.fori_loop(0, rows // (group_bands * BR), pixels, 0)
 
     i0 = iota((nz * n4, 1), 0)
     row_slot = (((i0 % n4) // hc) * (nz * cap) + (i0 // n4) * cap + i0 % hc).astype(F32)
@@ -249,53 +268,70 @@
     look[1:2, :] = -sine * jnp.sin(heading) / (2.0 * CELL_SPACING)
     look[2:3, :] = jnp.cos(incidence)
 
-    loads[3].wait()
     loads[4].wait()
+
+    def unit_sums(i, j):
+        lane = iota((BR, 128), 1)
+        top = BR * i
+        at = slice(128 * j, 128 * j + 128)
+        around = epad[top : top + 32, 128 + 128 * j : 256 + 128 * j]
+        before, here, after = (
+            epad[top + 8 : top + 24, 128 * n : 128 * n + 128] for n in (j, j + 1, j + 2)
+        )
+        before = pltpu.roll(jnp.where(lane == 127, before, here), 1, 1)
+        after = pltpu.roll(jnp.where(lane == 0, after, here), 127, 1)
+        rise_cols = after - before
+        rise_rows = around[9:25] - around[7:23]
+        facing = look[2:3, at] - rise_cols * look[0:1, at] - rise_rows * look[1:2, at]
+        lit = (1 - layv[top : top + BR, at]).astype(F32)
+        unit = i * tiles + j
+        span = slice(8 * unit, 8 * unit + 8)
+        area = jnp.maximum(facing, 0.0) * lit
+        hist[span, :] = block_sums(area, places[span, :], low_table[unit])
+
+    nb = rows // BR
+    inside = [(i, j) for i in range(1, nb - 1) for j in range(1, tiles - 1)]
+    for i, j in inside:
+        unit_sums(i, j)
+
     for halo in halos:
         halo.wait_recv()
 
     @pl.when(r == 0)
     def _():
-        epad[0:8, 128 : 128 + cols] = jnp.zeros((8, cols), F32)
+        epad[0:8, inner] = jnp.zeros((8, cols), F32)
 
     @pl.when(r == nr - 1)
     def _():
-        epad[rows + 8 : rows + 16, 128 : 128 + cols] = jnp.zeros((8, cols), F32)
-
-    @pl.when((c == 0) & (s == 0))
-    def _():
-        epad[8 : 8 + rows, 0:128] = jnp.zeros((rows, 128), F32)
-
-    @pl.when((c == nz - 1) & (s == 1))
-    def _():
-        epad[8 : 8 + rows, 128 + cols : 256 + cols] = jnp.zeros((rows, 128), F32)
-
-    def bands(i, carry):
-        lane = iota((BR, 128), 1)
-        for n in range(group_bands):
-            top = pl.multiple_of(i * (group_bands * BR) + n * BR, BR)
-            around = epad[pl.ds(top, 32), 128 : 128 + cols]
-            mid = epad[pl.ds(pl.multiple_of(top + 8, 8), BR), :]
-            mids = [mid[:, 128 * j : 128 * j + 128] for j in range(tiles + 2)]
-            right = [pltpu.roll(x, 1, 1) for x in mids[:-1]]
-            left = [pltpu.roll(x, 127, 1) for x in mids[1:]]
-            for j in range(tiles):
-                at = slice(128 * j, 128 * j + 128)
-                unit = i * (group_bands * tiles) + n * tiles + j
-                span = pl.ds(pl.multiple_of(8 * unit, 8), 8)
-                before = jnp.where(lane == 0, right[j], right[j + 1])
-                after = jnp.where(lane == 127, left[j + 1], left[j])
-                rise_cols = after - before
-                rise_rows = around[9:25, at] - around[7:23, at]
-                facing = (
-                    look[2:3, at] - rise_cols * look[0:1, at] - rise_rows * look[1:2, at]
-                )
-                lit = (1 - layv[pl.ds(top, BR), at]).astype(F32)
-                area = jnp.maximum(facing, 0.0) * lit
-                hist[span, :] = block_sums(area, places[span, :], low_table[unit])
-        return carry
-
-    lax.fori_loop(0, rows // (group_bands * BR), bands, 0)
+        epad[rows + 8 : rows + 16, inner] = jnp.zeros((8, cols), F32)
+
+    first, last = (c == 0) & (s == 0), (c == nz - 1) & (s == 1)
+    west_edge = jnp.where(first, 0.0, edge_in[1, 7:8, :])
+    east_edge = jnp.where(last, 0.0, edge_in[0, 0:1, :])
+    epad[8 : 8 + rows, 0:128] = jnp.transpose(jnp.broadcast_to(west_edge, (128, rows)))
+    epad[8 : 8 + rows, 128 + cols : 256 + cols] = jnp.transpose(
+        jnp.broadcast_to(east_edge, (128, rows))
+    )
+    for i in range(nb):
+        for j in range(tiles):
+            if (i, j) not in inside:
+                unit_sums(i, j)
+
+    done(idrecv.at[0 : nr - 1], id_recv)
+    names = idrecv[0]
+    for i in range(1, nr):
+        names = names + idrecv[i]
+    named[0] = names
+    tells = [
+        pltpu.make_async_remote_copy(
+            src_ref=named.at[0], dst_ref=named.at[n + 1],
+            send_sem=name_send.at[n], recv_sem=name_recv.at[n],
+            device_id={"mapcol": plane(step)}, device_id_type=MESH,
+        )
+        for n, step in enumerate((1, -1, 2, -2))
+    ]
+    for tell in tells:
+        tell.start()
 
     left = iota((nz * n4, 128), 1) < 64
     sums = hist[...]
@@ -323,16 +359,14 @@
         ).astype(BF16)
 
     loads[5].wait()
-    done(idrecv.at[:, 3:nz], id_recv.at[1])
-    done(idrecv.at[0 : nr - 1, 0:3], id_recv.at[0])
-    names = idrecv[0]
-    for i in range(1, nr):
-        names = names + idrecv[i]
+    for tell in tells:
+        tell.wait_recv()
+    from_step = (0, 0, 0, 1, 1, 2, 2)
     lane = iota((1, 128), 1)
     even = ((lane % n4) // hc + r) % 2 == 0
     for t, table in enumerate(TABLES):
         for m, p in enumerate(table):
-            name = names[p : p + 1, :]
+            name = named[from_step[p] if p < 7 else 3 + t, p : p + 1, :]
             if p == 7:
                 name = jnp.where(even == (t == 0), name, -1.0)
             if 2 * n4 < 128:
@@ -434,8 +468,9 @@
 
     for halo in halos:
         halo.wait_send()
-    done(idsend.at[:, 3:nz], id_send.at[1])
-    done(idsend.at[0 : nr - 1, 0:3], id_send.at[0])
+    done(idsend.at[0 : nr - 1], id_send)
+    for tell in tells:
+        tell.wait_send()
     for q in range(2):
         done_rows(sendb.at[q], out_send.at[q])
         done_rows(backb.at[q], ret_send.at[q])
@@ -502,10 +537,13 @@
             pltpu.VMEM((3, 128, 3 * 128), BF16),
             pltpu.VMEM((3, 3 * 128, 128), BF16),
             pltpu.VMEM((tb, PIX), F32),
+            pltpu.VMEM((2, 8, rows), F32),
+            pltpu.VMEM((2, 8, rows), F32),
             pltpu.VMEM((2, nz, n4, 128), F32),
             pltpu.VMEM((2, nz, n4, 128), F32),
             pltpu.VMEM((nr, nz, 128), F32),
             pltpu.VMEM((nr, nz, 128), F32),
+            pltpu.VMEM((5, nz, 128), F32),
             pltpu.VMEM((2, 2, 64, 128), F32),
             pltpu.VMEM((2, 2, 64, 128), F32),
             pltpu.VMEM((2, 64, 128), F32),
@@ -515,8 +553,10 @@
             dma((6,)),
             dma((4,)),
             dma((4,)),
-            dma((2,)),
-            dma((2,)),
+            dma,
+            dma,
+            dma((4,)),
+            dma((4,)),
             *([dma((2, 2))] * 8),
         ],
         compiler_params=pltpu.CompilerParams(

time: 49.3 us -> 45.9 us (0.931)
  Pallas kernels: 48.2 us -> 45.1 us
    pallas_call x1, Pallas kernels: 46.7 us -> 43.6 us  [per_device(): pl.pallas_call(functools.partial(exchange, nr, nz, cap), out_shape=(jax.S...]
where the time goes in v4:
time: 45.9 us; the launch traced here: 45.7 us
  Pallas kernels  45.1 us (98%)
  between operations  0.64 us (1%)
    pallas_call x1, Pallas kernels, per_device(): pl.pallas_call(functools.partial(exchange, nr, nz, cap), out_shape=(jax.S...  43.6 us
    pallas_call x1, Pallas kernels, per_device(): pl.pallas_call(lookup, out_shape=(jax.ShapeDtypeStruct((held, PIX), F32),...  1.45 us

profile of v4, /device:TPU:32, one launch (start us, length us, event | category | flops | bytes accessed | tf_op | source)
XLA Modules:
  0.0 45.7 jit_solution(12404677676379580885)
XLA Ops:
  0.6 43.6 %shard_map.77 = (f32[128,128]{1,0:T(8,128)S(1)}, f32[512,128]{1,0:T(8,128)S(1)}, s32[512,256]{1,0:T(8,128)S(1)}) custom-call(f32[256,512]{1,0:T(8,128)} %elev.1, s32[256,512]{1,0:T(8,128)} %lay.1, s32[256,512]{1,0:T(8,128)} %pix.1, s32[1,512]{1,0:T(1,128)} %bitcast.1, s32[1,512]{1,0:T(1,128)} %local_in.1, f32[128,128]{1,0:T(8,128)} %back_in.1), custom_call_target="tpu_custom_call" | custom-call | tf_op jit(solution)/shard_map/pallas_call | solution.py:516
  44.3 1.4 %shard_map.78 = (f32[128,128]{1,0:T(8,128)}, f32[256,512]{1,0:T(8,128)}) custom-call(f32[512,128]{1,0:T(8,128)S(1)} %get-tuple-element.5.found, s32[512,256]{1,0:T(8,128)S(1)} %get-tuple-element.6.places, f32[128,128]{1,0:T(8,128)S(1)} %get-tuple-element.7.gamma), custom_call_target="tpu_custom_call" | custom-call | tf_op jit(solution)/shard_map/pallas_call | solution.py:574

commit v5 on v4

--- a/solution.py
+++ b/solution.py
@@ -82,7 +82,11 @@
 
 
 STEP = (0, 2, -2, 1, 3, -1, -3, 4)
-SPANS = ((3, 5, 1), (5, 7, -1), (7, 8, 2), (0, 3, 0))
+SPANS = ((7, 8, 2), (3, 5, 1), (5, 7, -1), (0, 3, 0))
+AWAY = (
+    (2, 2), (1, 3), (3, 1), (2, 1), (1, 2), (3, 3), (1, 1), (2, 3),
+    (3, 2), (2, 0), (0, 2), (1, 0), (3, 0), (0, 1), (0, 3), (0, 0),
+)
 TABLES = ((1, 4, 7), (2, 6, 7), (0, 3, 5))
 
 
@@ -92,7 +96,7 @@
     gamma, found, places,
     target, local, back, low_table, epad, layv, pixv, look, put_low, put_high, pick, oht, oh, hist,
     edge_out, edge_in, sendb, recvb, idsend, idrecv, named, partial, cin, packed, gin, backb, retb,
-    in_sem, halo_send, halo_recv, id_send, id_recv, name_send, name_recv, out_send, out_recv,
+    plane_sem, steps_sem, in_sem, halo_send, halo_recv, id_send, id_recv, name_send, name_recv, out_send, out_recv,
     sum_send, sum_recv, gam_send, gam_recv, ret_send, ret_recv,
 ):
     rows, cols = elev.shape
@@ -106,14 +110,15 @@
     def plane(step):
         return lax.rem(c + (step + nz), nz)
 
-    def peer_of(i):
-        if nr != 16:
-            return lax.rem(r + 1 + i, nr)
-
-        def away(n):
-            return jnp.where(n == 0, 2, jnp.where(n == 3, 0, 2 * n - 1))
-
-        return (r // 4 + away(i // 4)) % 4 * 4 + (r % 4 + away(i % 4)) % 4
+    if nr == 16:
+        along_x = [(r // 4 + n) % 4 * 4 for n in range(4)]
+        along_y = [(r % 4 + n) % 4 for n in range(4)]
+        peers = [along_x[x] + along_y[y] for x, y in AWAY]
+        line_x = [along_x[n] + along_y[0] for n in (2, 1, 3)]
+        line_y = [along_x[0] + along_y[n] for n in (2, 1, 3)]
+    else:
+        peers = [lax.rem(r + 1 + i, nr) for i in range(nr)]
+        line_x, line_y = [], peers[:-1]
 
     west = {"mapcol": lax.rem(c + nz - 1 + s, nz), "sect": 1 - s}
     east = {"mapcol": lax.rem(c + s, nz), "sect": 1 - s}
@@ -121,25 +126,16 @@
 
     barrier = pltpu.get_barrier_semaphore()
 
-    def greet(j, carry):
-        peer = peer_of(j)
-        for step in (2, -2, 1, -1):
-            pl.semaphore_signal(
-                barrier, inc=1, device_id={"maprow": peer, "mapcol": plane(step)},
-                device_id_type=MESH,
-            )
-        return carry
-
-    def greet_plane(j, carry):
-        pl.semaphore_signal(
-            barrier, inc=1, device_id={"maprow": peer_of(j)}, device_id_type=MESH
-        )
-        return carry
-
-    for neighbour in (west, east):
-        pl.semaphore_signal(barrier, inc=1, device_id=neighbour, device_id_type=MESH)
-    lax.fori_loop(0, nr, greet, 0)
-    lax.fori_loop(0, nr - 1, greet_plane, 0)
+    line_x = [{"maprow": i} for i in line_x]
+    line_y = [{"maprow": i} for i in line_y]
+    line_z = [{"mapcol": plane(step)} for step in (2, -2, 1, -1)]
+    greeted = (north, south, west, east, *line_z, *line_x, *line_y)
+
+    def greet(devices, sem):
+        for device in devices:
+            pl.semaphore_signal(sem, inc=1, device_id=device, device_id_type=MESH)
+
+    greet(greeted, barrier)
 
     loads = [
         pltpu.make_async_copy(target_in, target, in_sem.at[0]),
@@ -173,26 +169,11 @@
     idsend[...] = dot_nt(ids, lanes).reshape(nr, nz, 128)
     idrecv[pl.ds(r, 1)] = idsend[pl.ds(r, 1)]
 
-    loads[2].wait()
-    group_bands = 8 if rows % (8 * BR) == 0 else 2
-
-    def pixels(i, carry):
-        for n in range(group_bands):
-            top = pl.multiple_of(i * (group_bands * BR) + n * BR, BR)
-            for j in range(tiles):
-                unit = i * (group_bands * tiles) + n * tiles + j
-                place, low = pixel_side(pixv[pl.ds(top, BR), 128 * j : 128 * j + 128])
-                places[pl.ds(pl.multiple_of(8 * unit, 8), 8), :] = place
-                low_table[unit] = low
-        return carry
-
-    lax.fori_loop(0, rows // (group_bands * BR), pixels, 0)
-
     loads[3].wait()
     edge_out[0] = jnp.transpose(epad[8 : 8 + rows, 128:256])[0:8]
     edge_out[1] = jnp.transpose(epad[8 : 8 + rows, cols : 128 + cols])[120:128]
 
-    pl.semaphore_wait(barrier, 5 * nr - 1 + 2)
+    pl.semaphore_wait(barrier, len(greeted))
 
     inner = slice(128, 128 + cols)
     halos = [
@@ -210,16 +191,32 @@
     ]
     for halo in halos:
         halo.start()
-
-    def name_slots(i, carry):
-        peer = peer_of(i)
+    greet(line_x, plane_sem)
+
+    loads[2].wait()
+    group_bands = 8 if rows % (8 * BR) == 0 else 2
+
+    def pixels(i, carry):
+        for n in range(group_bands):
+            top = pl.multiple_of(i * (group_bands * BR) + n * BR, BR)
+            for j in range(tiles):
+                unit = i * (group_bands * tiles) + n * tiles + j
+                place, low = pixel_side(pixv[pl.ds(top, BR), 128 * j : 128 * j + 128])
+                places[pl.ds(pl.multiple_of(8 * unit, 8), 8), :] = place
+                low_table[unit] = low
+        return carry
+
+    lax.fori_loop(0, rows // (group_bands * BR), pixels, 0)
+
+    if line_x:
+        pl.semaphore_wait(plane_sem, len(line_x))
+    greet(line_z, steps_sem)
+
+    for peer in peers[:-1]:
         pltpu.make_async_remote_copy(
             src_ref=idsend.at[peer], dst_ref=idrecv.at[r], send_sem=id_send, recv_sem=id_recv,
             device_id={"maprow": peer}, device_id_type=MESH,
         ).start()
-        return carry
-
-    lax.fori_loop(0, nr - 1, name_slots, 0)
 
     def to_peers(source, sink, send_sem, recv_sem, way):
         def start(span, peer):
@@ -234,17 +231,10 @@
                 device_id={"maprow": peer, "mapcol": where}, device_id_type=MESH,
             ).start()
 
-        def far(j, carry):
-            for span in SPANS[:3]:
-                start(span, peer_of(j))
-            return carry
-
-        def near(j, carry):
-            start(SPANS[3], peer_of(j))
-            return carry
-
-        lax.fori_loop(0, nr, far, 0)
-        lax.fori_loop(0, nr - 1, near, 0)
+        for i, peer in enumerate(peers):
+            for span in SPANS:
+                if i < nr - 1 or span[2] != 0:
+                    start(span, peer)
 
     def done(part, sem):
         pltpu.make_async_copy(part, part, sem).wait()
@@ -317,21 +307,7 @@
             if (i, j) not in inside:
                 unit_sums(i, j)
 
-    done(idrecv.at[0 : nr - 1], id_recv)
-    names = idrecv[0]
-    for i in range(1, nr):
-        names = names + idrecv[i]
-    named[0] = names
-    tells = [
-        pltpu.make_async_remote_copy(
-            src_ref=named.at[0], dst_ref=named.at[n + 1],
-            send_sem=name_send.at[n], recv_sem=name_recv.at[n],
-            device_id={"mapcol": plane(step)}, device_id_type=MESH,
-        )
-        for n, step in enumerate((1, -1, 2, -2))
-    ]
-    for tell in tells:
-        tell.start()
+    pl.semaphore_wait(steps_sem, len(line_z))
 
     left = iota((nz * n4, 128), 1) < 64
     sums = hist[...]
@@ -343,6 +319,24 @@
     for q in range(2):
         recvb[q, 0:3, mine] = sendb[q, 0:3, mine]
         to_peers(of_rows(sendb.at[q]), of_rows(recvb.at[q]), out_send.at[q], out_recv.at[q], 1)
+        if q == 1:
+            break
+
+        done(idrecv.at[0 : nr - 1], id_recv)
+        names = idrecv[0]
+        for i in range(1, nr):
+            names = names + idrecv[i]
+        named[0] = names
+        tells = [
+            pltpu.make_async_remote_copy(
+                src_ref=named.at[0], dst_ref=named.at[n + 1],
+                send_sem=name_send.at[n], recv_sem=name_recv.at[n],
+                device_id={"mapcol": plane(step)}, device_id_type=MESH,
+            )
+            for n, step in enumerate((1, -1, 2, -2))
+        ]
+        for tell in tells:
+            tell.start()
 
     row_of = (
         within
@@ -365,17 +359,23 @@
     lane = iota((1, 128), 1)
     even = ((lane % n4) // hc + r) % 2 == 0
     for t, table in enumerate(TABLES):
+        asked = []
         for m, p in enumerate(table):
             name = named[from_step[p] if p < 7 else 3 + t, p : p + 1, :]
             if p == 7:
                 name = jnp.where(even == (t == 0), name, -1.0)
+            asked.append(name)
             if 2 * n4 < 128:
                 name = jnp.where(lane < 2 * n4, name, -1.0)
             wide = jnp.broadcast_to(name, (128, 128))
             at = slice(128 * m, 128 * m + 128)
-            oht[t, :, at] = jnp.where(wide == iotaf((128, 128), 0), 1.0, 0.0).astype(BF16)
             oh[t, at, :] = jnp.where(
                 jnp.transpose(wide) == iotaf((128, 128), 1), 1.0, 0.0
+            ).astype(BF16)
+        for half_at in range(2):
+            name = jnp.concatenate([x[:, n4 * half_at : n4 * half_at + n4] for x in asked], axis=1)
+            oht[t, 128 * half_at : 128 * half_at + 128, :] = jnp.where(
+                iotaf((128, 3 * n4), 0) == name, 1.0, 0.0
             ).astype(BF16)
     half = iota((64, 128), 1) < 64
     backs = [back[0:64, :], back[64:128, :]]
@@ -384,19 +384,15 @@
         jnp.where(half, pltpu.roll(backs[0], 64, 1), backs[1]),
     ]
 
-    def filled(x):
-        if 2 * n4 == 128:
-            return x
-        return jnp.concatenate([x, jnp.zeros((128 - 2 * n4, 128), F32)], axis=0)
+    whole_half = iota((128, 128), 1) < 64
 
     def table_of(q, t):
-        given = []
-        for p in TABLES[t]:
-            x = recvb[q, p]
-            y = pltpu.roll(x, 64, 1)
-            given.append(split(filled(jnp.concatenate([x, y] if q == 0 else [y, x], axis=0))))
-        total = folded(dot(oht[t], jnp.concatenate(given, axis=0)))
-        return jnp.where(half, total[0:64], pltpu.roll(total[64:128], 64, 1))
+        given = jnp.concatenate([split(recvb[q, p]) for p in TABLES[t]], axis=0)
+        both = folded(dot(oht[t], given))
+        low, high = both[0:128], both[128:256]
+        total = jnp.where(whole_half, low, high) if q == 0 else jnp.where(whole_half, high, low)
+        total = total + pltpu.roll(total, 64, 1)
+        return jnp.where(half, total[0:64], total[64:128])
 
     def two_steps(source, sink, send_sem, recv_sem, way):
         return pltpu.make_async_remote_copy(
@@ -484,15 +480,15 @@
     chunk = 64 if rows % 64 == 0 else rows
     copies = [pltpu.make_async_copy(gamma, gamma_out, sems.at[0])]
     copies[0].start()
-    for unit in range(rows // BR * tiles):
-        span = slice(8 * unit, 8 * unit + 8)
-        for half in range(2):
-            place = places[span, 128 * half : 128 * half + 128]
-            top, at = BR * (unit // tiles) + 8 * half, 128 * (unit % tiles)
-            cells[top : top + 8, at : at + 128] = jnp.take_along_axis(
-                found[span, :], place, axis=1
-            )
     for k in range(rows // chunk):
+        for unit in range(k * (chunk // BR) * tiles, (k + 1) * (chunk // BR) * tiles):
+            span = slice(8 * unit, 8 * unit + 8)
+            for half in range(2):
+                place = places[span, 128 * half : 128 * half + 128]
+                top, at = BR * (unit // tiles) + 8 * half, 128 * (unit % tiles)
+                cells[top : top + 8, at : at + 128] = jnp.take_along_axis(
+                    found[span, :], place, axis=1
+                )
         for top in range(k * chunk, (k + 1) * chunk, 8):
             for at in range(0, cols, 128):
                 piece = (slice(top, top + 8), slice(at, at + 128))
@@ -534,7 +530,7 @@
             pltpu.VMEM((nz * n4, tb), BF16),
             pltpu.VMEM((nz * n4, tb), BF16),
             pltpu.VMEM((tb, nz * n4), BF16),
-            pltpu.VMEM((3, 128, 3 * 128), BF16),
+            pltpu.VMEM((3, 256, 3 * n4), BF16),
             pltpu.VMEM((3, 3 * 128, 128), BF16),
             pltpu.VMEM((tb, PIX), F32),
             pltpu.VMEM((2, 8, rows), F32),
@@ -550,6 +546,8 @@
             pltpu.VMEM((2, 2, 64, 128), F32),
             pltpu.VMEM((2, nz, n4, 128), F32),
             pltpu.VMEM((2, nz, n4, 128), F32),
+            pltpu.SemaphoreType.REGULAR,
+            pltpu.SemaphoreType.REGULAR,
             dma((6,)),
             dma((4,)),
             dma((4,)),

time: 45.9 us -> 43.9 us (0.956)
  Pallas kernels: 45.1 us -> 43.1 us
    pallas_call x1, Pallas kernels: 43.6 us -> 41.7 us  [per_device(): pl.pallas_call(functools.partial(exchange, nr, nz, cap), out_shape=(jax.S...]
where the time goes in v5:
time: 43.9 us; the launch traced here: 43.8 us
  Pallas kernels  43.1 us (98%)
  between operations  0.64 us (1%)
    pallas_call x1, Pallas kernels, per_device(): pl.pallas_call(functools.partial(exchange, nr, nz, cap), out_shape=(jax.S...  41.7 us
    pallas_call x1, Pallas kernels, per_device(): pl.pallas_call(lookup, out_shape=(jax.ShapeDtypeStruct((held, PIX), F32),...  1.49 us

profile of v5, /device:TPU:32, one launch (start us, length us, event | category | flops | bytes accessed | tf_op | source)
XLA Modules:
  0.0 43.8 jit_solution(8948157954809564244)
XLA Ops:
  0.6 41.7 %shard_map.77 = (f32[128,128]{1,0:T(8,128)S(1)}, f32[512,128]{1,0:T(8,128)S(1)}, s32[512,256]{1,0:T(8,128)S(1)}) custom-call(f32[256,512]{1,0:T(8,128)} %elev.1, s32[256,512]{1,0:T(8,128)} %lay.1, s32[256,512]{1,0:T(8,128)} %pix.1, s32[1,512]{1,0:T(1,128)} %bitcast.1, s32[1,512]{1,0:T(1,128)} %local_in.1, f32[128,128]{1,0:T(8,128)} %back_in.1), custom_call_target="tpu_custom_call" | custom-call | tf_op jit(solution)/shard_map/pallas_call | solution.py:512
  42.3 1.5 %shard_map.78 = (f32[128,128]{1,0:T(8,128)}, f32[256,512]{1,0:T(8,128)}) custom-call(f32[512,128]{1,0:T(8,128)S(1)} %get-tuple-element.5.found, s32[512,256]{1,0:T(8,128)S(1)} %get-tuple-element.6.places, f32[128,128]{1,0:T(8,128)S(1)} %get-tuple-element.7.gamma), custom_call_target="tpu_custom_call" | custom-call | tf_op jit(solution)/shard_map/pallas_call | solution.py:572

commit v6 on v5

--- a/solution.py
+++ b/solution.py
@@ -177,10 +177,10 @@
 
     inner = slice(128, 128 + cols)
     halos = [
-        (epad.at[rows : rows + 8, inner], epad.at[0:8, inner], south),
-        (epad.at[8:16, inner], epad.at[rows + 8 : rows + 16, inner], north),
-        (edge_out.at[0], edge_in.at[0], west),
-        (edge_out.at[1], edge_in.at[1], east),
+        (epad.at[rows + 7 : rows + 8, inner], epad.at[7:8, inner], south),
+        (epad.at[8:9, inner], epad.at[rows + 8 : rows + 9, inner], north),
+        (edge_out.at[0, 0:1], edge_in.at[0, 0:1], west),
+        (edge_out.at[1, 7:8], edge_in.at[1, 7:8], east),
     ]
     halos = [
         pltpu.make_async_remote_copy(
@@ -289,11 +289,11 @@
 
     @pl.when(r == 0)
     def _():
-        epad[0:8, inner] = jnp.zeros((8, cols), F32)
+        epad[7:8, inner] = jnp.zeros((1, cols), F32)
 
     @pl.when(r == nr - 1)
     def _():
-        epad[rows + 8 : rows + 16, inner] = jnp.zeros((8, cols), F32)
+        epad[rows + 8 : rows + 9, inner] = jnp.zeros((1, cols), F32)
 
     first, last = (c == 0) & (s == 0), (c == nz - 1) & (s == 1)
     west_edge = jnp.where(first, 0.0, edge_in[1, 7:8, :])
@@ -319,24 +319,22 @@
     for q in range(2):
         recvb[q, 0:3, mine] = sendb[q, 0:3, mine]
         to_peers(of_rows(sendb.at[q]), of_rows(recvb.at[q]), out_send.at[q], out_recv.at[q], 1)
-        if q == 1:
-            break
-
-        done(idrecv.at[0 : nr - 1], id_recv)
-        names = idrecv[0]
-        for i in range(1, nr):
-            names = names + idrecv[i]
-        named[0] = names
-        tells = [
-            pltpu.make_async_remote_copy(
-                src_ref=named.at[0], dst_ref=named.at[n + 1],
-                send_sem=name_send.at[n], recv_sem=name_recv.at[n],
-                device_id={"mapcol": plane(step)}, device_id_type=MESH,
-            )
-            for n, step in enumerate((1, -1, 2, -2))
-        ]
-        for tell in tells:
-            tell.start()
+
+    done(idrecv.at[0 : nr - 1], id_recv)
+    names = idrecv[0]
+    for i in range(1, nr):
+        names = names + idrecv[i]
+    named[0] = names
+    tells = [
+        pltpu.make_async_remote_copy(
+            src_ref=named.at[0], dst_ref=named.at[n + 1],
+            send_sem=name_send.at[n], recv_sem=name_recv.at[n],
+            device_id={"mapcol": plane(step)}, device_id_type=MESH,
+        )
+        for n, step in enumerate((1, -1, 2, -2))
+    ]
+    for tell in tells:
+        tell.start()
 
     row_of = (
         within
@@ -443,6 +441,7 @@
     for q in range(2):
         for p, x in zip(TABLES[2], served(q, 2)):
             backb[q, p] = x
+    for q in range(2):
         gammas[2 * q].wait_recv()
         gammas[2 * q + 1].wait_recv()
         ahead_rows, behind_rows = served(q, 0), served(q, 1)

time: 43.9 us -> 43.1 us (0.982)
  Pallas kernels: 43.1 us -> 42.3 us
    pallas_call x1, Pallas kernels: 41.7 us -> 40.8 us  [per_device(): pl.pallas_call(functools.partial(exchange, nr, nz, cap), out_shape=(jax.S...]
where the time goes in v6:
time: 43.1 us; the launch traced here: 42.9 us
  Pallas kernels  42.3 us (98%)
  between operations  0.64 us (1%)
    pallas_call x1, Pallas kernels, per_device(): pl.pallas_call(functools.partial(exchange, nr, nz, cap), out_shape=(jax.S...  40.8 us
    pallas_call x1, Pallas kernels, per_device(): pl.pallas_call(lookup, out_shape=(jax.ShapeDtypeStruct((held, PIX), F32),...  1.49 us

profile of v6, /device:TPU:32, one launch (start us, length us, event | category | flops | bytes accessed | tf_op | source)
XLA Modules:
  0.0 42.9 jit_solution(5483890704185192913)
XLA Ops:
  0.6 40.8 %shard_map.77 = (f32[128,128]{1,0:T(8,128)S(1)}, f32[512,128]{1,0:T(8,128)S(1)}, s32[512,256]{1,0:T(8,128)S(1)}) custom-call(f32[256,512]{1,0:T(8,128)} %elev.1, s32[256,512]{1,0:T(8,128)} %lay.1, s32[256,512]{1,0:T(8,128)} %pix.1, s32[1,512]{1,0:T(1,128)} %bitcast.1, s32[1,512]{1,0:T(1,128)} %local_in.1, f32[128,128]{1,0:T(8,128)} %back_in.1), custom_call_target="tpu_custom_call" | custom-call | tf_op jit(solution)/shard_map/pallas_call | solution.py:511
  41.5 1.5 %shard_map.78 = (f32[128,128]{1,0:T(8,128)}, f32[256,512]{1,0:T(8,128)}) custom-call(f32[512,128]{1,0:T(8,128)S(1)} %get-tuple-element.5.found, s32[512,256]{1,0:T(8,128)S(1)} %get-tuple-element.6.places, f32[128,128]{1,0:T(8,128)S(1)} %get-tuple-element.7.gamma), custom_call_target="tpu_custom_call" | custom-call | tf_op jit(solution)/shard_map/pallas_call | solution.py:571

commit v7 on v6

--- a/solution.py
+++ b/solution.py
@@ -145,8 +145,8 @@
         pltpu.make_async_copy(lay, layv, in_sem.at[4]),
         pltpu.make_async_copy(back_in, back, in_sem.at[5]),
     ]
-    for load in loads:
-        load.start()
+    for i in (0, 1, 3, 2, 4, 5):
+        loads[i].start()
 
     loads[0].wait()
     loads[1].wait()

time: 43.1 us -> 43 us (level)
  no operation moved by 1% of the time
where the time goes in v7:
time: 43 us; the launch traced here: 42.9 us
  Pallas kernels  42.3 us (98%)
  between operations  0.64 us (1%)
    pallas_call x1, Pallas kernels, per_device(): pl.pallas_call(functools.partial(exchange, nr, nz, cap), out_shape=(jax.S...  40.8 us
    pallas_call x1, Pallas kernels, per_device(): pl.pallas_call(lookup, out_shape=(jax.ShapeDtypeStruct((held, PIX), F32),...  1.49 us

profile of v7, /device:TPU:32, one launch (start us, length us, event | category | flops | bytes accessed | tf_op | source)
XLA Modules:
  0.0 42.9 jit_solution(4642154655880353274)
XLA Ops:
  0.6 40.8 %shard_map.77 = (f32[128,128]{1,0:T(8,128)S(1)}, f32[512,128]{1,0:T(8,128)S(1)}, s32[512,256]{1,0:T(8,128)S(1)}) custom-call(f32[256,512]{1,0:T(8,128)} %elev.1, s32[256,512]{1,0:T(8,128)} %lay.1, s32[256,512]{1,0:T(8,128)} %pix.1, s32[1,512]{1,0:T(1,128)} %bitcast.1, s32[1,512]{1,0:T(1,128)} %local_in.1, f32[128,128]{1,0:T(8,128)} %back_in.1), custom_call_target="tpu_custom_call" | custom-call | tf_op jit(solution)/shard_map/pallas_call | solution.py:511
  41.5 1.5 %shard_map.78 = (f32[128,128]{1,0:T(8,128)}, f32[256,512]{1,0:T(8,128)}) custom-call(f32[512,128]{1,0:T(8,128)S(1)} %get-tuple-element.5.found, s32[512,256]{1,0:T(8,128)S(1)} %get-tuple-element.6.places, f32[128,128]{1,0:T(8,128)S(1)} %get-tuple-element.7.gamma), custom_call_target="tpu_custom_call" | custom-call | tf_op jit(solution)/shard_map/pallas_call | solution.py:571
